TPU v7x, 512 devices: a whole 4x8x8 slice. The times are simulated.
512 devices in a mesh: grp: 16 (over x, z_hi, core), ctx: 32 (over y, z_lo).
Axes of the slice: x: 4, y: 8, z: 8 (z_hi: 2, z_lo: 4; z = z_hi * 4 + z_lo), core: 2. Of those that a mesh axis runs over, the one named last changes fastest.
Arguments:
- queries: bfloat16 [8192, 4096], P('ctx', 'grp'), may hold values from -4 to 4
- keys: bfloat16 [8192, 512], P('ctx'), may hold values from -4 to 4
- values: bfloat16 [8192, 512], P('ctx'), may hold values from -6 to 6
- attn_gate: bfloat16 [8192, 4096], P('ctx', 'grp'), may hold values from -6 to 6
- delta_query: bfloat16 [8192, 2048], P('ctx', 'grp'), may hold values from -6 to 6
- delta_key: bfloat16 [8192, 2048], P('ctx', 'grp'), may hold values from -6 to 6
- delta_value: bfloat16 [8192, 4096], P('ctx', 'grp'), may hold values from -6 to 6
- delta_gate: bfloat16 [8192, 4096], P('ctx', 'grp'), may hold values from -6 to 6
- decay_log: float32 [32, 8192], P('grp', 'ctx'), may hold values from -0.7 to 0
- beta: float32 [32, 8192], P('grp', 'ctx'), may hold values from 0.005 to 0.9
- norm_gain: float32 [128], replicated, may hold values from 0.1 to 1.9
- attn_out_weight: bfloat16 [4096, 2048], P('grp'), may hold values from -0.125 to 0.125
- delta_out_weight: bfloat16 [4096, 2048], P('grp'), may hold values from -0.125 to 0.125
- doc_lengths: int32 [4], replicated, may hold values from 1 to 64, 128 in all
Outputs:
- attn_mixed: bfloat16 [8192, 2048], P('ctx', 'grp')
- delta_mixed: bfloat16 [8192, 2048], P('ctx', 'grp')
Inputs may be any that keep to these rules, and one draw needn't show every extreme that they name: `doc_lengths`: lengths of the 4 prompts in order along the sequence, counted in blocks of 64 tokens; they cover the whole sequence and the longest covers exactly half of its blocks.
All inputs are finite; a program needn't handle non-finite values.
Results may differ from a plain program's by a relative error of at most 0.023.
Values may be sent and summed in bfloat16 or wider, within the bound.
A program may use at most 64 MiB of HBM per device.

v0:
```python
import jax
import jax.numpy as jnp
from jax import lax
from jax.sharding import PartitionSpec as P

HEADS = 16
HD = 256
KVH = 2
DHD = 128
BLOCK = 64


epsilon = 1e-06
masked_score = -1e30
highest = lax.Precision.HIGHEST


def from_behind(block, axis, distance):
    devices = range(lax.axis_size(axis))
    route = [(i - distance, i) for i in devices if i - distance in devices]
    return lax.ppermute(block, axis, route)


def prompt_index(positions, prompt_ends):
    return jnp.sum((positions[:, None] >= prompt_ends[None, :]).astype(jnp.int32), axis=1)


def matmul_heads(left_side, right_side):
    return jnp.einsum("hij,hjk->hik", left_side, right_side, precision=highest)


def gated_norm(core_out, gate_input, norm_gain):
    squares = jnp.mean(core_out * core_out, axis=-1, keepdims=True)
    normed = core_out * lax.rsqrt(squares + epsilon) * norm_gain
    gate_value = gate_input.astype(jnp.float32).reshape(core_out.shape)
    gated = (normed * jax.nn.silu(gate_value)).astype(jnp.bfloat16)
    return gated.reshape(core_out.shape[0], core_out.shape[1] * core_out.shape[2])


def by_block(array):
    return jnp.moveaxis(array, 1, 0)


def rounded_term(product):
    return lax.optimization_barrier(product.astype(jnp.bfloat16)).astype(jnp.float32)


def local(
    queries,
    keys,
    values,
    attn_gate,
    delta_query,
    delta_key,
    delta_value,
    delta_gate,
    decay_log,
    beta,
    norm_gain,
    attn_out_weight,
    delta_out_weight,
    doc_lengths,
):
    tok_rows = queries.shape[0]
    ctx_count = lax.axis_size("ctx")
    ctx_place = lax.axis_index("ctx")
    grp_place = lax.axis_index("grp")
    local_heads = queries.shape[1] // HD
    kv_head = grp_place * local_heads // (HEADS // KVH)
    own_kv = jnp.stack(
        [
            lax.dynamic_slice_in_dim(keys, kv_head * HD, HD, 1),
            lax.dynamic_slice_in_dim(values, kv_head * HD, HD, 1),
        ]
    )
    prompt_ends = jnp.cumsum(doc_lengths) * BLOCK
    token_pos = ctx_place * tok_rows + jnp.arange(tok_rows, dtype=jnp.int32)
    query_pos = jnp.tile(token_pos, local_heads)
    query_doc = prompt_index(query_pos, prompt_ends)
    query_rows = (
        queries.reshape(tok_rows, local_heads, HD)
        .transpose(1, 0, 2)
        .reshape(local_heads * tok_rows, HD)
    )
    score_scale = HD ** (-0.5)

    def attend(partial_value, kv_block, key_pos):
        running_max, running_sum, running_acc = partial_value
        scores = (
            lax.dot_general(
                query_rows,
                kv_block[0],
                (((1,), (1,)), ((), ())),
                preferred_element_type=jnp.float32,
            )
            * score_scale
        )
        key_doc = prompt_index(key_pos, prompt_ends)
        allowed = (
            (key_pos[None, :] >= 0)
            & (key_pos[None, :] <= query_pos[:, None])
            & (key_doc[None, :] == query_doc[:, None])
        )
        scores = jnp.where(allowed, scores, masked_score)
        new_max = jnp.maximum(running_max, jnp.max(scores, axis=1))
        weights = jnp.where(allowed, jnp.exp(scores - new_max[:, None]), 0.0)
        rescale = jnp.exp(running_max - new_max)
        new_sum = running_sum * rescale + jnp.sum(weights, axis=1)
        new_acc = running_acc * rescale[:, None] + jnp.dot(
            weights.astype(jnp.bfloat16), kv_block[1], preferred_element_type=jnp.float32
        )
        return (new_max, new_sum, new_acc)

    start_carry = (
        jnp.full((local_heads * tok_rows,), masked_score, jnp.float32),
        jnp.zeros((local_heads * tok_rows,), jnp.float32),
        jnp.zeros((local_heads * tok_rows, HD), jnp.float32),
    )
    own_carry = attend(start_carry, own_kv, token_pos)

    def pass_step(turn_index, looped):
        partial_value, moving = looped
        moving = from_behind(moving, "ctx", 1)
        owner = ctx_place - turn_index
        key_pos = owner * tok_rows + jnp.arange(tok_rows, dtype=jnp.int32)
        return (attend(partial_value, moving, key_pos), moving)

    final_carry, _ = lax.fori_loop(1, ctx_count, pass_step, (own_carry, own_kv))
    attn_core = final_carry[2] / final_carry[1][:, None]
    attn_core = (
        attn_core.reshape(local_heads, tok_rows, HD)
        .transpose(1, 0, 2)
        .reshape(tok_rows, local_heads * HD)
    )
    attn_heads = (attn_core * jax.nn.sigmoid(attn_gate.astype(jnp.float32))).astype(jnp.bfloat16)
    value_heads = delta_value.shape[1] // DHD
    key_heads = delta_key.shape[1] // DHD
    share_ratio = value_heads // key_heads
    block_count = tok_rows // BLOCK

    def unit_heads(inputs):
        shaped = inputs.astype(jnp.float32).reshape(tok_rows, key_heads, DHD)
        shaped = shaped * lax.rsqrt(jnp.sum(shaped * shaped, axis=-1, keepdims=True) + epsilon)
        return jnp.repeat(shaped.transpose(1, 0, 2), share_ratio, axis=0).reshape(
            value_heads, block_count, BLOCK, DHD
        )

    query_unit = unit_heads(delta_query)
    key_unit = unit_heads(delta_key)
    value_rows = (
        delta_value.astype(jnp.float32)
        .reshape(tok_rows, value_heads, DHD)
        .transpose(1, 0, 2)
        .reshape(value_heads, block_count, BLOCK, DHD)
    )
    log_cum = jnp.cumsum(decay_log.reshape(value_heads, block_count, BLOCK), axis=-1)
    growth = jnp.exp(log_cum)
    lower_mask = jnp.tril(jnp.ones((BLOCK, BLOCK), jnp.bool_))
    strict_mask = jnp.tril(jnp.ones((BLOCK, BLOCK), jnp.bool_), -1)
    log_diff = log_cum[..., :, None] - log_cum[..., None, :]
    decay_mat = jnp.where(lower_mask, jnp.exp(jnp.where(lower_mask, log_diff, 0.0)), 0.0)
    beta_rows = beta.reshape(value_heads, block_count, BLOCK)
    key_inner = jnp.einsum("hnid,hnjd->hnij", key_unit, key_unit, precision=highest)
    strict_part = jnp.where(strict_mask, beta_rows[..., :, None] * decay_mat * key_inner, 0.0)
    right_side = jnp.concatenate(
        [(beta_rows * growth)[..., None] * key_unit, beta_rows[..., None] * value_rows], axis=-1
    )
    solved = lax.linalg.triangular_solve(
        strict_part, right_side, left_side=True, lower=True, unit_diagonal=True
    )
    weight_keys = solved[..., :DHD]
    new_values = solved[..., DHD:]
    inner_mat = jnp.einsum("hnid,hnjd->hnij", query_unit, key_unit, precision=highest) * decay_mat
    query_eff = growth[..., None] * query_unit - jnp.einsum(
        "hnij,hnjd->hnid", inner_mat, weight_keys, precision=highest
    )
    local_out = jnp.einsum("hnij,hnjd->hnid", inner_mat, new_values, precision=highest)
    tail_decay = jnp.exp(log_cum[..., -1:] - log_cum)
    keys_tail = key_unit * tail_decay[..., None]
    doc_starts = jnp.cumsum(doc_lengths) - doc_lengths
    block_index = ctx_place * block_count + jnp.arange(block_count, dtype=jnp.int32)
    keep_block = 1.0 - jnp.any(block_index[:, None] == doc_starts[None, :], axis=1).astype(
        jnp.float32
    )
    identity_mat = jnp.eye(DHD, dtype=jnp.float32)
    transition = growth[..., -1][..., None, None] * identity_mat - jnp.einsum(
        "hnci,hncj->hnij", keys_tail, weight_keys, precision=highest
    )
    transition = transition * keep_block[None, :, None, None]
    offsets = jnp.einsum("hnci,hncj->hnij", keys_tail, new_values, precision=highest)

    def compose(carried, entries):
        return (
            (
                matmul_heads(entries[0], carried[0]),
                matmul_heads(entries[0], carried[1]) + entries[1],
            ),
            None,
        )

    eye_heads = jnp.broadcast_to(identity_mat, (value_heads, DHD, DHD))
    zero_state = jnp.zeros((value_heads, DHD, DHD), jnp.float32)
    (device_map, device_offset), _ = lax.scan(
        compose, (eye_heads, zero_state), (by_block(transition), by_block(offsets))
    )

    def chain_step(turn_index, incoming):
        return from_behind(
            (matmul_heads(device_map, incoming) + device_offset).astype(jnp.bfloat16), "ctx", 1
        ).astype(jnp.float32)

    start_state = lax.fori_loop(0, ctx_count - 1, chain_step, zero_state)

    def advance(carried, entries):
        query_blk, local_blk, trans_blk, offset_blk, keep_value = entries
        entry_state = carried * keep_value
        produced = jnp.einsum("hcd,hde->hce", query_blk, entry_state, precision=highest) + local_blk
        return (matmul_heads(trans_blk, carried) + offset_blk, produced)

    _, produced = lax.scan(
        advance,
        start_state,
        (
            by_block(query_eff),
            by_block(local_out),
            by_block(transition),
            by_block(offsets),
            keep_block,
        ),
    )
    core_out = jnp.moveaxis(produced, 0, 1).reshape(value_heads, tok_rows, DHD).transpose(1, 0, 2)
    delta_heads = gated_norm(core_out, delta_gate, norm_gain)
    columns = attn_out_weight
    attn_mixed = (
        lax.psum_scatter(
            rounded_term(
                lax.dot_general(
                    columns,
                    attn_heads,
                    (((0,), (1,)), ((), ())),
                    preferred_element_type=jnp.float32,
                )
            ).astype(jnp.bfloat16),
            "grp",
            scatter_dimension=0,
            tiled=True,
        )
        .astype(jnp.float32)
        .T.astype(jnp.bfloat16)
    )
    columns = delta_out_weight
    delta_mixed = (
        lax.psum_scatter(
            rounded_term(
                lax.dot_general(
                    columns,
                    delta_heads,
                    (((0,), (1,)), ((), ())),
                    preferred_element_type=jnp.float32,
                )
            ).astype(jnp.bfloat16),
            "grp",
            scatter_dimension=0,
            tiled=True,
        )
        .astype(jnp.float32)
        .T.astype(jnp.bfloat16)
    )
    return (attn_mixed, delta_mixed)


def solution(mesh):
    placed = (
        P("ctx", "grp"),
        P("ctx", None),
        P("ctx", None),
        P("ctx", "grp"),
        P("ctx", "grp"),
        P("ctx", "grp"),
        P("ctx", "grp"),
        P("ctx", "grp"),
        P("grp", "ctx"),
        P("grp", "ctx"),
        P(),
        P("grp", None),
        P("grp", None),
        P(),
    )
    return jax.shard_map(
        local,
        mesh=mesh,
        in_specs=placed,
        out_specs=(P("ctx", "grp"), P("ctx", "grp")),
        check_vma=False,
    )
```

profile of v0, /device:TPU:56, one launch (start us, length us, event | category | flops | bytes accessed | tf_op | source)
XLA Modules:
  0.0 973.7 jit_solution(10565096881565021722)
XLA Ops:
  13.0 39.3 %custom-call.3 = f32[2,4,1,64,64]{3,4,2,1,0:T(8,128)S(1)} custom-call(f32[2,4,1,64,64]{4,3,2,1,0:T(8,128)S(1)} %fusion.45), custom_call_target="InvertDiagBlocksLowerTriangular" | custom-call | tf_op jit(solution)/shard_map/triangular_solve | solution.py:168
  60.1 288.1 %while.59 = (s32[]{:T(128)}, f32[2,128,128]{2,1,0:T(8,128)S(1)}, f32[2,128,128]{2,1,0:T(8,128)S(1)}, f32[2,128,128]{2,1,0:T(8,128)S(1)}, s32[]{:T(128)}, /*index=5*/s32[]{:T(128)}) while((s32[]{:T(128)}, f32[2,128,128]{2,1,0:T(8,128)S(1)}, f32[2,128,128]{2,1,0:T(8,128)S(1)}, f32[2,128,128]{2,1,0:T(8,128)S(1)}, s32[]{:T(128)}, ...), condition=%wide.region_16.17_spmd.clone, body=%wide.region_15.16_spmd.clone.sunk | while | flops 50462720 | bytes 917623 | solution.py:212
  361.1 454.8 %while.57 = (s32[]{:T(128)}, f32[256]{0:T(256)S(1)}, f32[256]{0:T(256)S(1)}, f32[256,256]{1,0:T(8,128)}, bf16[2,256,256]{2,1,0:T(8,128)(2,1)S(1)}, /*index=5*/s3...) while((s32[]{:T(128)}, f32[256]{0:T(256)S(1)}, ...), condition=%wide.region_8.9_spmd.clone, body=%wide.region_4.8_spmd.clone.sunk | while | flops 68620544 | bytes 3311313 | solution.py:128
  363.3 10.8 %collective-permute-done = bf16[2,256,256]{2,1,0:T(8,128)(2,1)S(1)} collective-permute-done((bf16[2,256,256]{2,1,0:T(8,128)(2,1)S(1)}, bf16[2,256,256]{2,1,0:T(8,128)(2,1)S(1)}, u32[]{:S(2)}, u32[]{:S(2)}) %collective-permute-start) | collective-permute-done | bytes 262176 | tf_op jit(solution)/shard_map/while/body/eval_jaxpr/ppermute | solution.py:21
  378.7 11.5 %collective-permute-done = bf16[2,256,256]{2,1,0:T(8,128)(2,1)S(1)} collective-permute-done((bf16[2,256,256]{2,1,0:T(8,128)(2,1)S(1)}, bf16[2,256,256]{2,1,0:T(8,128)(2,1)S(1)}, u32[]{:S(2)}, u32[]{:S(2)}) %collective-permute-start) | collective-permute-done | bytes 262176 | tf_op jit(solution)/shard_map/while/body/eval_jaxpr/ppermute | solution.py:21
  394.8 10.6 %collective-permute-done = bf16[2,256,256]{2,1,0:T(8,128)(2,1)S(1)} collective-permute-done((bf16[2,256,256]{2,1,0:T(8,128)(2,1)S(1)}, bf16[2,256,256]{2,1,0:T(8,128)(2,1)S(1)}, u32[]{:S(2)}, u32[]{:S(2)}) %collective-permute-start) | collective-permute-done | bytes 262176 | tf_op jit(solution)/shard_map/while/body/eval_jaxpr/ppermute | solution.py:21
  410.0 9.7 collective-permute-done
  424.3 8.9 collective-permute-done
  437.8 9.1 collective-permute-done
  451.5 8.9 collective-permute-done
  465.0 8.9 collective-permute-done
  478.5 8.9 collective-permute-done
  492.1 8.9 collective-permute-done
  505.6 8.9 collective-permute-done
  519.1 12.4 %collective-permute-done = bf16[2,256,256]{2,1,0:T(8,128)(2,1)S(1)} collective-permute-done((bf16[2,256,256]{2,1,0:T(8,128)(2,1)S(1)}, bf16[2,256,256]{2,1,0:T(8,128)(2,1)S(1)}, u32[]{:S(2)}, u32[]{:S(2)}) %collective-permute-start) | collective-permute-done | bytes 262176 | tf_op jit(solution)/shard_map/while/body/eval_jaxpr/ppermute | solution.py:21
  536.1 10.1 %collective-permute-done = bf16[2,256,256]{2,1,0:T(8,128)(2,1)S(1)} collective-permute-done((bf16[2,256,256]{2,1,0:T(8,128)(2,1)S(1)}, bf16[2,256,256]{2,1,0:T(8,128)(2,1)S(1)}, u32[]{:S(2)}, u32[]{:S(2)}) %collective-permute-start) | collective-permute-done | bytes 262176 | tf_op jit(solution)/shard_map/while/body/eval_jaxpr/ppermute | solution.py:21
  550.8 13.2 %collective-permute-done = bf16[2,256,256]{2,1,0:T(8,128)(2,1)S(1)} collective-permute-done((bf16[2,256,256]{2,1,0:T(8,128)(2,1)S(1)}, bf16[2,256,256]{2,1,0:T(8,128)(2,1)S(1)}, u32[]{:S(2)}, u32[]{:S(2)}) %collective-permute-start) | collective-permute-done | bytes 262176 | tf_op jit(solution)/shard_map/while/body/eval_jaxpr/ppermute | solution.py:21
  568.6 8.9 collective-permute-done
  622.6 9.9 %collective-permute-done = bf16[2,256,256]{2,1,0:T(8,128)(2,1)S(1)} collective-permute-done((bf16[2,256,256]{2,1,0:T(8,128)(2,1)S(1)}, bf16[2,256,256]{2,1,0:T(8,128)(2,1)S(1)}, u32[]{:S(2)}, u32[]{:S(2)}) %collective-permute-start) | collective-permute-done | bytes 262176 | tf_op jit(solution)/shard_map/while/body/eval_jaxpr/ppermute | solution.py:21
  637.0 11.2 %collective-permute-done = bf16[2,256,256]{2,1,0:T(8,128)(2,1)S(1)} collective-permute-done((bf16[2,256,256]{2,1,0:T(8,128)(2,1)S(1)}, bf16[2,256,256]{2,1,0:T(8,128)(2,1)S(1)}, u32[]{:S(2)}, u32[]{:S(2)}) %collective-permute-start) | collective-permute-done | bytes 262176 | tf_op jit(solution)/shard_map/while/body/eval_jaxpr/ppermute | solution.py:21
  652.9 13.1 %collective-permute-done = bf16[2,256,256]{2,1,0:T(8,128)(2,1)S(1)} collective-permute-done((bf16[2,256,256]{2,1,0:T(8,128)(2,1)S(1)}, bf16[2,256,256]{2,1,0:T(8,128)(2,1)S(1)}, u32[]{:S(2)}, u32[]{:S(2)}) %collective-permute-start) | collective-permute-done | bytes 262176 | tf_op jit(solution)/shard_map/while/body/eval_jaxpr/ppermute | solution.py:21
  670.6 12.6 %collective-permute-done = bf16[2,256,256]{2,1,0:T(8,128)(2,1)S(1)} collective-permute-done((bf16[2,256,256]{2,1,0:T(8,128)(2,1)S(1)}, bf16[2,256,256]{2,1,0:T(8,128)(2,1)S(1)}, u32[]{:S(2)}, u32[]{:S(2)}) %collective-permute-start) | collective-permute-done | bytes 262176 | tf_op jit(solution)/shard_map/while/body/eval_jaxpr/ppermute | solution.py:21
  687.7 10.8 %collective-permute-done = bf16[2,256,256]{2,1,0:T(8,128)(2,1)S(1)} collective-permute-done((bf16[2,256,256]{2,1,0:T(8,128)(2,1)S(1)}, bf16[2,256,256]{2,1,0:T(8,128)(2,1)S(1)}, u32[]{:S(2)}, u32[]{:S(2)}) %collective-permute-start) | collective-permute-done | bytes 262176 | tf_op jit(solution)/shard_map/while/body/eval_jaxpr/ppermute | solution.py:21
  703.1 11.1 %collective-permute-done = bf16[2,256,256]{2,1,0:T(8,128)(2,1)S(1)} collective-permute-done((bf16[2,256,256]{2,1,0:T(8,128)(2,1)S(1)}, bf16[2,256,256]{2,1,0:T(8,128)(2,1)S(1)}, u32[]{:S(2)}, u32[]{:S(2)}) %collective-permute-start) | collective-permute-done | bytes 262176 | tf_op jit(solution)/shard_map/while/body/eval_jaxpr/ppermute | solution.py:21
  718.8 9.3 collective-permute-done
  732.7 10.0 %collective-permute-done = bf16[2,256,256]{2,1,0:T(8,128)(2,1)S(1)} collective-permute-done((bf16[2,256,256]{2,1,0:T(8,128)(2,1)S(1)}, bf16[2,256,256]{2,1,0:T(8,128)(2,1)S(1)}, u32[]{:S(2)}, u32[]{:S(2)}) %collective-permute-start) | collective-permute-done | bytes 262176 | tf_op jit(solution)/shard_map/while/body/eval_jaxpr/ppermute | solution.py:21
  747.3 11.0 %collective-permute-done = bf16[2,256,256]{2,1,0:T(8,128)(2,1)S(1)} collective-permute-done((bf16[2,256,256]{2,1,0:T(8,128)(2,1)S(1)}, bf16[2,256,256]{2,1,0:T(8,128)(2,1)S(1)}, u32[]{:S(2)}, u32[]{:S(2)}) %collective-permute-start) | collective-permute-done | bytes 262176 | tf_op jit(solution)/shard_map/while/body/eval_jaxpr/ppermute | solution.py:21
  762.9 9.3 collective-permute-done
  776.7 9.2 collective-permute-done
  790.5 8.9 collective-permute-done
  804.0 9.3 collective-permute-done
  820.3 145.0 %reduce-scatter.7.cloned.1.call-done = bf16[128,256]{1,0:T(8,128)(2,1)} async-done(((bf16[2048,256]{1,0:T(8,128)(2,1)}), bf16[128,256]{1,0:T(8,128)(2,1)}) %reduce-scatter.7.cloned.1.call-update) | async-done | bytes 65552
  (586 shorter events, 496.2 us)
Async XLA Ops:
  7.2 811.5 %reduce-scatter.9.cloned.1.call-start = ((), (), s32[]{:S(2)}) async-start(), calls=%async_computation.3 | async-start | bytes 1114112
  358.4 606.9 %reduce-scatter.7.cloned.1.call-start = ((), (), s32[]{:S(2)}) async-start(), calls=%async_computation.2 | async-start | bytes 1114112
  361.1 13.0 %collective-permute-start = (bf16[2,256,256]{2,1,0:T(8,128)(2,1)S(1)}, bf16[2,256,256]{2,1,0:T(8,128)(2,1)S(1)}, u32[]{:S(2)}, u32[]{:S(2)}) collective-permute-start(bf16[2,256,256]{2,1,0:T(8,128)(2,1)S(1)} %get-tuple-element.662), channel_id=1, source_target_pairs={{0,1},{1,2},{2,3},{3,4},{4,5},{5,6},{6,7},{7,8},{8,9},{9,10},{10,1... | collective-permute-start | bytes 786440 | tf_op jit(solution)/shard_map/while/body/eval_jaxpr/ppermute | solution.py:21
  376.7 13.5 %collective-permute-start = (bf16[2,256,256]{2,1,0:T(8,128)(2,1)S(1)}, bf16[2,256,256]{2,1,0:T(8,128)(2,1)S(1)}, u32[]{:S(2)}, u32[]{:S(2)}) collective-permute-start(bf16[2,256,256]{2,1,0:T(8,128)(2,1)S(1)} %get-tuple-element.662), channel_id=1, source_target_pairs={{0,1},{1,2},{2,3},{3,4},{4,5},{5,6},{6,7},{7,8},{8,9},{9,10},{10,1... | collective-permute-start | bytes 786440 | tf_op jit(solution)/shard_map/while/body/eval_jaxpr/ppermute | solution.py:21
  392.7 12.6 %collective-permute-start = (bf16[2,256,256]{2,1,0:T(8,128)(2,1)S(1)}, bf16[2,256,256]{2,1,0:T(8,128)(2,1)S(1)}, u32[]{:S(2)}, u32[]{:S(2)}) collective-permute-start(bf16[2,256,256]{2,1,0:T(8,128)(2,1)S(1)} %get-tuple-element.662), channel_id=1, source_target_pairs={{0,1},{1,2},{2,3},{3,4},{4,5},{5,6},{6,7},{7,8},{8,9},{9,10},{10,1... | collective-permute-start | bytes 786440 | tf_op jit(solution)/shard_map/while/body/eval_jaxpr/ppermute | solution.py:21
  407.9 11.8 %collective-permute-start = (bf16[2,256,256]{2,1,0:T(8,128)(2,1)S(1)}, bf16[2,256,256]{2,1,0:T(8,128)(2,1)S(1)}, u32[]{:S(2)}, u32[]{:S(2)}) collective-permute-start(bf16[2,256,256]{2,1,0:T(8,128)(2,1)S(1)} %get-tuple-element.662), channel_id=1, source_target_pairs={{0,1},{1,2},{2,3},{3,4},{4,5},{5,6},{6,7},{7,8},{8,9},{9,10},{10,1... | collective-permute-start | bytes 786440 | tf_op jit(solution)/shard_map/while/body/eval_jaxpr/ppermute | solution.py:21
  422.3 11.0 %collective-permute-start = (bf16[2,256,256]{2,1,0:T(8,128)(2,1)S(1)}, bf16[2,256,256]{2,1,0:T(8,128)(2,1)S(1)}, u32[]{:S(2)}, u32[]{:S(2)}) collective-permute-start(bf16[2,256,256]{2,1,0:T(8,128)(2,1)S(1)} %get-tuple-element.662), channel_id=1, source_target_pairs={{0,1},{1,2},{2,3},{3,4},{4,5},{5,6},{6,7},{7,8},{8,9},{9,10},{10,1... | collective-permute-start | bytes 786440 | tf_op jit(solution)/shard_map/while/body/eval_jaxpr/ppermute | solution.py:21
  435.8 11.2 %collective-permute-start = (bf16[2,256,256]{2,1,0:T(8,128)(2,1)S(1)}, bf16[2,256,256]{2,1,0:T(8,128)(2,1)S(1)}, u32[]{:S(2)}, u32[]{:S(2)}) collective-permute-start(bf16[2,256,256]{2,1,0:T(8,128)(2,1)S(1)} %get-tuple-element.662), channel_id=1, source_target_pairs={{0,1},{1,2},{2,3},{3,4},{4,5},{5,6},{6,7},{7,8},{8,9},{9,10},{10,1... | collective-permute-start | bytes 786440 | tf_op jit(solution)/shard_map/while/body/eval_jaxpr/ppermute | solution.py:21
  449.5 11.0 %collective-permute-start = (bf16[2,256,256]{2,1,0:T(8,128)(2,1)S(1)}, bf16[2,256,256]{2,1,0:T(8,128)(2,1)S(1)}, u32[]{:S(2)}, u32[]{:S(2)}) collective-permute-start(bf16[2,256,256]{2,1,0:T(8,128)(2,1)S(1)} %get-tuple-element.662), channel_id=1, source_target_pairs={{0,1},{1,2},{2,3},{3,4},{4,5},{5,6},{6,7},{7,8},{8,9},{9,10},{10,1... | collective-permute-start | bytes 786440 | tf_op jit(solution)/shard_map/while/body/eval_jaxpr/ppermute | solution.py:21
  463.0 11.0 %collective-permute-start = (bf16[2,256,256]{2,1,0:T(8,128)(2,1)S(1)}, bf16[2,256,256]{2,1,0:T(8,128)(2,1)S(1)}, u32[]{:S(2)}, u32[]{:S(2)}) collective-permute-start(bf16[2,256,256]{2,1,0:T(8,128)(2,1)S(1)} %get-tuple-element.662), channel_id=1, source_target_pairs={{0,1},{1,2},{2,3},{3,4},{4,5},{5,6},{6,7},{7,8},{8,9},{9,10},{10,1... | collective-permute-start | bytes 786440 | tf_op jit(solution)/shard_map/while/body/eval_jaxpr/ppermute | solution.py:21
  476.5 11.0 %collective-permute-start = (bf16[2,256,256]{2,1,0:T(8,128)(2,1)S(1)}, bf16[2,256,256]{2,1,0:T(8,128)(2,1)S(1)}, u32[]{:S(2)}, u32[]{:S(2)}) collective-permute-start(bf16[2,256,256]{2,1,0:T(8,128)(2,1)S(1)} %get-tuple-element.662), channel_id=1, source_target_pairs={{0,1},{1,2},{2,3},{3,4},{4,5},{5,6},{6,7},{7,8},{8,9},{9,10},{10,1... | collective-permute-start | bytes 786440 | tf_op jit(solution)/shard_map/while/body/eval_jaxpr/ppermute | solution.py:21
  490.0 11.0 %collective-permute-start = (bf16[2,256,256]{2,1,0:T(8,128)(2,1)S(1)}, bf16[2,256,256]{2,1,0:T(8,128)(2,1)S(1)}, u32[]{:S(2)}, u32[]{:S(2)}) collective-permute-start(bf16[2,256,256]{2,1,0:T(8,128)(2,1)S(1)} %get-tuple-element.662), channel_id=1, source_target_pairs={{0,1},{1,2},{2,3},{3,4},{4,5},{5,6},{6,7},{7,8},{8,9},{9,10},{10,1... | collective-permute-start | bytes 786440 | tf_op jit(solution)/shard_map/while/body/eval_jaxpr/ppermute | solution.py:21
  503.5 11.0 %collective-permute-start = (bf16[2,256,256]{2,1,0:T(8,128)(2,1)S(1)}, bf16[2,256,256]{2,1,0:T(8,128)(2,1)S(1)}, u32[]{:S(2)}, u32[]{:S(2)}) collective-permute-start(bf16[2,256,256]{2,1,0:T(8,128)(2,1)S(1)} %get-tuple-element.662), channel_id=1, source_target_pairs={{0,1},{1,2},{2,3},{3,4},{4,5},{5,6},{6,7},{7,8},{8,9},{9,10},{10,1... | collective-permute-start | bytes 786440 | tf_op jit(solution)/shard_map/while/body/eval_jaxpr/ppermute | solution.py:21
  517.0 14.5 %collective-permute-start = (bf16[2,256,256]{2,1,0:T(8,128)(2,1)S(1)}, bf16[2,256,256]{2,1,0:T(8,128)(2,1)S(1)}, u32[]{:S(2)}, u32[]{:S(2)}) collective-permute-start(bf16[2,256,256]{2,1,0:T(8,128)(2,1)S(1)} %get-tuple-element.662), channel_id=1, source_target_pairs={{0,1},{1,2},{2,3},{3,4},{4,5},{5,6},{6,7},{7,8},{8,9},{9,10},{10,1... | collective-permute-start | bytes 786440 | tf_op jit(solution)/shard_map/while/body/eval_jaxpr/ppermute | solution.py:21
  534.1 12.2 %collective-permute-start = (bf16[2,256,256]{2,1,0:T(8,128)(2,1)S(1)}, bf16[2,256,256]{2,1,0:T(8,128)(2,1)S(1)}, u32[]{:S(2)}, u32[]{:S(2)}) collective-permute-start(bf16[2,256,256]{2,1,0:T(8,128)(2,1)S(1)} %get-tuple-element.662), channel_id=1, source_target_pairs={{0,1},{1,2},{2,3},{3,4},{4,5},{5,6},{6,7},{7,8},{8,9},{9,10},{10,1... | collective-permute-start | bytes 786440 | tf_op jit(solution)/shard_map/while/body/eval_jaxpr/ppermute | solution.py:21
  548.8 15.2 %collective-permute-start = (bf16[2,256,256]{2,1,0:T(8,128)(2,1)S(1)}, bf16[2,256,256]{2,1,0:T(8,128)(2,1)S(1)}, u32[]{:S(2)}, u32[]{:S(2)}) collective-permute-start(bf16[2,256,256]{2,1,0:T(8,128)(2,1)S(1)} %get-tuple-element.662), channel_id=1, source_target_pairs={{0,1},{1,2},{2,3},{3,4},{4,5},{5,6},{6,7},{7,8},{8,9},{9,10},{10,1... | collective-permute-start | bytes 786440 | tf_op jit(solution)/shard_map/while/body/eval_jaxpr/ppermute | solution.py:21
  566.5 11.0 %collective-permute-start = (bf16[2,256,256]{2,1,0:T(8,128)(2,1)S(1)}, bf16[2,256,256]{2,1,0:T(8,128)(2,1)S(1)}, u32[]{:S(2)}, u32[]{:S(2)}) collective-permute-start(bf16[2,256,256]{2,1,0:T(8,128)(2,1)S(1)} %get-tuple-element.662), channel_id=1, source_target_pairs={{0,1},{1,2},{2,3},{3,4},{4,5},{5,6},{6,7},{7,8},{8,9},{9,10},{10,1... | collective-permute-start | bytes 786440 | tf_op jit(solution)/shard_map/while/body/eval_jaxpr/ppermute | solution.py:21
  580.0 11.0 %collective-permute-start = (bf16[2,256,256]{2,1,0:T(8,128)(2,1)S(1)}, bf16[2,256,256]{2,1,0:T(8,128)(2,1)S(1)}, u32[]{:S(2)}, u32[]{:S(2)}) collective-permute-start(bf16[2,256,256]{2,1,0:T(8,128)(2,1)S(1)} %get-tuple-element.662), channel_id=1, source_target_pairs={{0,1},{1,2},{2,3},{3,4},{4,5},{5,6},{6,7},{7,8},{8,9},{9,10},{10,1... | collective-permute-start | bytes 786440 | tf_op jit(solution)/shard_map/while/body/eval_jaxpr/ppermute | solution.py:21
  593.5 11.0 %collective-permute-start = (bf16[2,256,256]{2,1,0:T(8,128)(2,1)S(1)}, bf16[2,256,256]{2,1,0:T(8,128)(2,1)S(1)}, u32[]{:S(2)}, u32[]{:S(2)}) collective-permute-start(bf16[2,256,256]{2,1,0:T(8,128)(2,1)S(1)} %get-tuple-element.662), channel_id=1, source_target_pairs={{0,1},{1,2},{2,3},{3,4},{4,5},{5,6},{6,7},{7,8},{8,9},{9,10},{10,1... | collective-permute-start | bytes 786440 | tf_op jit(solution)/shard_map/while/body/eval_jaxpr/ppermute | solution.py:21
  620.6 11.9 %collective-permute-start = (bf16[2,256,256]{2,1,0:T(8,128)(2,1)S(1)}, bf16[2,256,256]{2,1,0:T(8,128)(2,1)S(1)}, u32[]{:S(2)}, u32[]{:S(2)}) collective-permute-start(bf16[2,256,256]{2,1,0:T(8,128)(2,1)S(1)} %get-tuple-element.662), channel_id=1, source_target_pairs={{0,1},{1,2},{2,3},{3,4},{4,5},{5,6},{6,7},{7,8},{8,9},{9,10},{10,1... | collective-permute-start | bytes 786440 | tf_op jit(solution)/shard_map/while/body/eval_jaxpr/ppermute | solution.py:21
  635.0 13.3 %collective-permute-start = (bf16[2,256,256]{2,1,0:T(8,128)(2,1)S(1)}, bf16[2,256,256]{2,1,0:T(8,128)(2,1)S(1)}, u32[]{:S(2)}, u32[]{:S(2)}) collective-permute-start(bf16[2,256,256]{2,1,0:T(8,128)(2,1)S(1)} %get-tuple-element.662), channel_id=1, source_target_pairs={{0,1},{1,2},{2,3},{3,4},{4,5},{5,6},{6,7},{7,8},{8,9},{9,10},{10,1... | collective-permute-start | bytes 786440 | tf_op jit(solution)/shard_map/while/body/eval_jaxpr/ppermute | solution.py:21
  650.8 15.1 %collective-permute-start = (bf16[2,256,256]{2,1,0:T(8,128)(2,1)S(1)}, bf16[2,256,256]{2,1,0:T(8,128)(2,1)S(1)}, u32[]{:S(2)}, u32[]{:S(2)}) collective-permute-start(bf16[2,256,256]{2,1,0:T(8,128)(2,1)S(1)} %get-tuple-element.662), channel_id=1, source_target_pairs={{0,1},{1,2},{2,3},{3,4},{4,5},{5,6},{6,7},{7,8},{8,9},{9,10},{10,1... | collective-permute-start | bytes 786440 | tf_op jit(solution)/shard_map/while/body/eval_jaxpr/ppermute | solution.py:21
  668.5 14.6 %collective-permute-start = (bf16[2,256,256]{2,1,0:T(8,128)(2,1)S(1)}, bf16[2,256,256]{2,1,0:T(8,128)(2,1)S(1)}, u32[]{:S(2)}, u32[]{:S(2)}) collective-permute-start(bf16[2,256,256]{2,1,0:T(8,128)(2,1)S(1)} %get-tuple-element.662), channel_id=1, source_target_pairs={{0,1},{1,2},{2,3},{3,4},{4,5},{5,6},{6,7},{7,8},{8,9},{9,10},{10,1... | collective-permute-start | bytes 786440 | tf_op jit(solution)/shard_map/while/body/eval_jaxpr/ppermute | solution.py:21
  685.7 12.8 %collective-permute-start = (bf16[2,256,256]{2,1,0:T(8,128)(2,1)S(1)}, bf16[2,256,256]{2,1,0:T(8,128)(2,1)S(1)}, u32[]{:S(2)}, u32[]{:S(2)}) collective-permute-start(bf16[2,256,256]{2,1,0:T(8,128)(2,1)S(1)} %get-tuple-element.662), channel_id=1, source_target_pairs={{0,1},{1,2},{2,3},{3,4},{4,5},{5,6},{6,7},{7,8},{8,9},{9,10},{10,1... | collective-permute-start | bytes 786440 | tf_op jit(solution)/shard_map/while/body/eval_jaxpr/ppermute | solution.py:21
  701.1 13.2 %collective-permute-start = (bf16[2,256,256]{2,1,0:T(8,128)(2,1)S(1)}, bf16[2,256,256]{2,1,0:T(8,128)(2,1)S(1)}, u32[]{:S(2)}, u32[]{:S(2)}) collective-permute-start(bf16[2,256,256]{2,1,0:T(8,128)(2,1)S(1)} %get-tuple-element.662), channel_id=1, source_target_pairs={{0,1},{1,2},{2,3},{3,4},{4,5},{5,6},{6,7},{7,8},{8,9},{9,10},{10,1... | collective-permute-start | bytes 786440 | tf_op jit(solution)/shard_map/while/body/eval_jaxpr/ppermute | solution.py:21
  716.8 11.3 %collective-permute-start = (bf16[2,256,256]{2,1,0:T(8,128)(2,1)S(1)}, bf16[2,256,256]{2,1,0:T(8,128)(2,1)S(1)}, u32[]{:S(2)}, u32[]{:S(2)}) collective-permute-start(bf16[2,256,256]{2,1,0:T(8,128)(2,1)S(1)} %get-tuple-element.662), channel_id=1, source_target_pairs={{0,1},{1,2},{2,3},{3,4},{4,5},{5,6},{6,7},{7,8},{8,9},{9,10},{10,1... | collective-permute-start | bytes 786440 | tf_op jit(solution)/shard_map/while/body/eval_jaxpr/ppermute | solution.py:21
  730.7 12.0 %collective-permute-start = (bf16[2,256,256]{2,1,0:T(8,128)(2,1)S(1)}, bf16[2,256,256]{2,1,0:T(8,128)(2,1)S(1)}, u32[]{:S(2)}, u32[]{:S(2)}) collective-permute-start(bf16[2,256,256]{2,1,0:T(8,128)(2,1)S(1)} %get-tuple-element.662), channel_id=1, source_target_pairs={{0,1},{1,2},{2,3},{3,4},{4,5},{5,6},{6,7},{7,8},{8,9},{9,10},{10,1... | collective-permute-start | bytes 786440 | tf_op jit(solution)/shard_map/while/body/eval_jaxpr/ppermute | solution.py:21
  745.2 13.0 %collective-permute-start = (bf16[2,256,256]{2,1,0:T(8,128)(2,1)S(1)}, bf16[2,256,256]{2,1,0:T(8,128)(2,1)S(1)}, u32[]{:S(2)}, u32[]{:S(2)}) collective-permute-start(bf16[2,256,256]{2,1,0:T(8,128)(2,1)S(1)} %get-tuple-element.662), channel_id=1, source_target_pairs={{0,1},{1,2},{2,3},{3,4},{4,5},{5,6},{6,7},{7,8},{8,9},{9,10},{10,1... | collective-permute-start | bytes 786440 | tf_op jit(solution)/shard_map/while/body/eval_jaxpr/ppermute | solution.py:21
  760.8 11.3 %collective-permute-start = (bf16[2,256,256]{2,1,0:T(8,128)(2,1)S(1)}, bf16[2,256,256]{2,1,0:T(8,128)(2,1)S(1)}, u32[]{:S(2)}, u32[]{:S(2)}) collective-permute-start(bf16[2,256,256]{2,1,0:T(8,128)(2,1)S(1)} %get-tuple-element.662), channel_id=1, source_target_pairs={{0,1},{1,2},{2,3},{3,4},{4,5},{5,6},{6,7},{7,8},{8,9},{9,10},{10,1... | collective-permute-start | bytes 786440 | tf_op jit(solution)/shard_map/while/body/eval_jaxpr/ppermute | solution.py:21
  774.7 11.2 %collective-permute-start = (bf16[2,256,256]{2,1,0:T(8,128)(2,1)S(1)}, bf16[2,256,256]{2,1,0:T(8,128)(2,1)S(1)}, u32[]{:S(2)}, u32[]{:S(2)}) collective-permute-start(bf16[2,256,256]{2,1,0:T(8,128)(2,1)S(1)} %get-tuple-element.662), channel_id=1, source_target_pairs={{0,1},{1,2},{2,3},{3,4},{4,5},{5,6},{6,7},{7,8},{8,9},{9,10},{10,1... | collective-permute-start | bytes 786440 | tf_op jit(solution)/shard_map/while/body/eval_jaxpr/ppermute | solution.py:21
  788.5 11.0 %collective-permute-start = (bf16[2,256,256]{2,1,0:T(8,128)(2,1)S(1)}, bf16[2,256,256]{2,1,0:T(8,128)(2,1)S(1)}, u32[]{:S(2)}, u32[]{:S(2)}) collective-permute-start(bf16[2,256,256]{2,1,0:T(8,128)(2,1)S(1)} %get-tuple-element.662), channel_id=1, source_target_pairs={{0,1},{1,2},{2,3},{3,4},{4,5},{5,6},{6,7},{7,8},{8,9},{9,10},{10,1... | collective-permute-start | bytes 786440 | tf_op jit(solution)/shard_map/while/body/eval_jaxpr/ppermute | solution.py:21
  802.0 11.4 %collective-permute-start = (bf16[2,256,256]{2,1,0:T(8,128)(2,1)S(1)}, bf16[2,256,256]{2,1,0:T(8,128)(2,1)S(1)}, u32[]{:S(2)}, u32[]{:S(2)}) collective-permute-start(bf16[2,256,256]{2,1,0:T(8,128)(2,1)S(1)} %get-tuple-element.662), channel_id=1, source_target_pairs={{0,1},{1,2},{2,3},{3,4},{4,5},{5,6},{6,7},{7,8},{8,9},{9,10},{10,1... | collective-permute-start | bytes 786440 | tf_op jit(solution)/shard_map/while/body/eval_jaxpr/ppermute | solution.py:21
  (43 other events, 1903.4 us)
Sparse Core Ops, SparseCore 0:
  358.6 132.7 reduce-scatter.8
  818.8 146.4 reduce-scatter.6
where the time goes:
time: 977 us; the launch traced here: 974 us
  waiting for transfers between devices  674 us (69%)
  starting transfers between devices  121 us (12%)
  matrix products  94.7 us (10%)
  other arithmetic  53.9 us (6%)
  between operations  14.5 us (1%)
  local copies, waits for them, and re-layouts  12.4 us (1%)
    ppermute x62, waiting for transfers between devices, from_behind(): return lax.ppermute(block, axis, route)  529 us
    unnamed x4, waiting for transfers between devices  145 us
    ppermute x62, starting transfers between devices, from_behind(): return lax.ppermute(block, axis, route)  121 us
    dot_general x32, matrix products, attend(): jnp.dot(weights.astype(jnp.bfloat16), kv_block[1], preferred_element_type...  64.7 us
    another operation x3, other arithmetic, local(): lax.linalg.triangular_solve(strict_part, right_side, left_side=True, lowe...  39.3 us
  transfers between devices with their start and end apart: 64, of which 63 were waited for; matrix products, arithmetic and copies ran while one was open for 9% of the time, Pallas kernels for 0%

commit v1 on v0

v1 whole, which is shorter than its diff:
```python
import functools

import jax
import jax.numpy as jnp
from jax import lax
from jax.experimental import pallas as pl
from jax.experimental.pallas import tpu as pltpu
from jax.sharding import PartitionSpec as P

MESH = pl.DeviceIdType.MESH
F32 = jnp.float32
BF16 = jnp.bfloat16

HEADS = 16
HD = 256
KVH = 2
DHD = 128
BLOCK = 64
TOK = 256
PIECE = 64
MSG = 2 * DHD + 16

EPS = 1e-06
MASKED = -2e30
START_MAX = -1e30

NT = (((1,), (1,)), ((), ()))
NN = (((1,), (0,)), ((), ()))


def dot(a, b, dims=NN):
    return lax.dot_general(a, b, dims, preferred_element_type=F32)


def split(x):
    high = x.astype(BF16)
    return high, (x - high.astype(F32)).astype(BF16)


def dot3(a, b):
    ah, al = a
    bh, bl = b
    return dot(ah, bh) + (dot(ah, bl) + dot(al, bh))


def dot2(a, b):
    return dot(a[0], b) + dot(a[1], b)


def kernel(
    ends_ref,
    q_ref,
    k_ref,
    v_ref,
    agate_ref,
    dq_ref,
    dk_ref,
    dv_ref,
    dgate_ref,
    decay_ref,
    beta_ref,
    gain_ref,
    wa_hbm,
    wd_hbm,
    oa_ref,
    od_ref,
    wa_ref,
    wd_ref,
    qall,
    kv,
    bias,
    acc,
    stat,
    accs,
    accr,
    stats,
    statr,
    own,
    csend,
    crecv,
    eff,
    pbuf,
    r1,
    s2,
    r2,
    s3,
    r3,
    w_sem,
    q_s,
    q_r,
    z_s,
    y_s,
    kv_r,
    c_s,
    c_r,
    a_s,
    a_r,
    t_s,
    t_r,
    s1_s,
    s1_r,
    s2_s,
    s2_r,
    s3_s,
    s3_r,
):
    grp = lax.axis_index("grp")
    ctx = lax.axis_index("ctx")
    x, zh, c = grp // 4, (grp // 2) % 2, grp % 2
    y, z = ctx // 4, ctx % 4
    xb = x % 2
    kvh = x // 2
    member = xb * 2 + c

    def grp_of(x_, zh_, c_):
        return x_ * 4 + zh_ * 2 + c_

    xn = x + 1 - 2 * xb
    quad = [(x, 1 - c), (xn, c), (xn, 1 - c)]
    quad_grp = [grp_of(a, zh, b) for a, b in quad]
    quad_member = [(a % 2) * 2 + b for a, b in quad]
    x_grp = [grp_of((x + d) % 4, zh, c) for d in (1, 2, 3)]
    z_grp = grp_of(x, 1 - zh, c)
    sib_grp = quad_grp[0]
    row_ctx = [y * 4 + (z + d) % 4 for d in (1, 2, 3)]

    def copy(src, dst, send, recv, g, r):
        return pltpu.make_async_remote_copy(
            src_ref=src,
            dst_ref=dst,
            send_sem=send,
            recv_sem=recv,
            device_id={"grp": g, "ctx": r},
            device_id_type=MESH,
        )

    def arrived(dst, sem):
        pltpu.make_async_copy(dst, dst, sem).wait()

    sends = []

    barrier = pltpu.get_barrier_semaphore()
    peers = [(g, ctx) for g in quad_grp + x_grp + [z_grp]]
    peers += [(grp, r) for r in row_ctx]
    peers += [(grp, (ctx + d) % 32) for d in (1, 31, 2, 30, 4, 28, 8, 24)]
    for g, r in peers:
        pl.semaphore_signal(barrier, inc=1, device_id={"grp": g, "ctx": r}, device_id_type=MESH)

    wa_copy = pltpu.make_async_copy(wa_hbm, wa_ref, w_sem.at[0])
    wd_copy = pltpu.make_async_copy(wd_hbm, wd_ref, w_sem.at[1])
    wa_copy.start()
    wd_copy.start()

    rows = pl.ds(pl.multiple_of(member * PIECE, PIECE), PIECE)
    cols = pl.ds(pl.multiple_of(kvh * HD, HD), HD)
    kv[0, 0, z] = k_ref[rows, cols]
    kv[0, 1, z] = v_ref[rows, cols]
    qall[member] = q_ref[...] * jnp.asarray(HD ** (-0.5), BF16)
    pl.semaphore_wait(barrier, len(peers))

    def forward(dy, zs):
        return copy(
            kv.at[dy, :, zs], kv.at[dy + 1, :, zs], y_s.at[dy * 4 + zs], kv_r.at[dy * 4 + 4 + zs], grp, ctx + 4
        )

    @pl.when(y < 7)
    def _():
        forward(0, z).start()

    for i in range(3):
        copy(kv.at[0, :, z], kv.at[0, :, z], z_s.at[i], kv_r.at[z], grp, row_ctx[i]).start()
    for i in (1, 2, 0):
        copy(qall.at[member], qall.at[member], q_s.at[i], q_r.at[i], quad_grp[i], ctx).start()

    ticks = [(dy, i) for dy in range(5) for i in range(4)][1:]

    def tick(count=1):
        for _ in range(count):
            if not ticks:
                return
            dy, i = ticks.pop(0)
            zs = (z + i) % 4

            @pl.when(y >= dy)
            def _():
                arrived(kv.at[dy, :, zs], kv_r.at[dy * 4 + zs])

                if dy < 4:

                    @pl.when(y < 7)
                    def _():
                        forward(dy, zs).start()

    def tick_through(dy):
        while ticks and ticks[0][0] <= dy:
            tick()

    first = ctx * TOK
    ends = [ends_ref[i] for i in range(4)]

    def prompt(pos):
        total = (pos >= ends[0]).astype(F32)
        for e in ends[1:]:
            total += (pos >= e).astype(F32)
        return total

    row_i = lax.broadcasted_iota(jnp.int32, (1, TOK), 1)
    col_i = lax.broadcasted_iota(jnp.int32, (TOK, 1), 0)
    pid_row = prompt(first + row_i)
    pid_col = prompt(first + col_i)
    pid_before = prompt(jnp.full((1, 1), first - 1, jnp.int32))
    pid_last = prompt(jnp.full((1, 1), first + TOK - 1, jnp.int32))

    ii = lax.broadcasted_iota(jnp.int32, (TOK, TOK), 0)
    jj = lax.broadcasted_iota(jnp.int32, (TOK, TOK), 1)
    lower = (jj <= ii) & (pid_col == pid_row)
    strict = jj < ii

    d0 = decay_ref[...]
    d_hi = d0.astype(BF16)
    rest = d0 - d_hi.astype(F32)
    d_mid = rest.astype(BF16)
    d_lo = (rest - d_mid.astype(F32)).astype(BF16)
    upper_ones = (ii <= jj).astype(F32).astype(BF16)
    pieces = jnp.concatenate([d_hi.astype(F32), d_mid.astype(F32), d_lo.astype(F32), jnp.zeros((10, TOK), F32)], axis=0)
    sums = dot(pieces.astype(BF16), upper_ones)
    cum = sums[0:2] + sums[2:4] + sums[4:6]

    kf = dk_ref[...].astype(F32)
    qf = dq_ref[...].astype(F32)
    rk_col = lax.rsqrt(jnp.sum(kf * kf, axis=1, keepdims=True) + EPS)
    rq_col = lax.rsqrt(jnp.sum(qf * qf, axis=1, keepdims=True) + EPS)
    rk_row = jnp.broadcast_to(rk_col, (TOK, DHD)).T[0:1]
    packed = jnp.concatenate([cum, beta_ref[...], jnp.zeros((DHD - 4, TOK), F32)], axis=0).T
    kk = dot(dk_ref[...], dk_ref[...], NT) * rk_col * rk_row
    qk = dot(dq_ref[...], dk_ref[...], NT) * rq_col * rk_row
    tick()

    decays, lows = [], []
    for h in range(2):
        diff = packed[:, h : h + 1] - cum[h : h + 1]
        decay = jnp.where(lower, jnp.exp(jnp.where(lower, diff, 0.0)), 0.0)
        decays.append(decay)
        lows.append(jnp.where(strict, packed[:, 2 + h : 3 + h] * decay * kk, 0.0))
    tick()

    eye = (ii == jj).astype(F32)
    inverses = None
    size = 1
    while size < TOK:
        cross = (ii // (2 * size) == jj // (2 * size)) & (ii // size != jj // size)
        if size == 1:
            inverses = [eye - jnp.where(cross, low, 0.0) for low in lows]
        else:
            parts = [split(t) for t in inverses]
            inner = [dot3(split(jnp.where(cross, low, 0.0)), t) for low, t in zip(lows, parts)]
            inverses = [t - dot3(tp, split(m)) for t, tp, m in zip(inverses, parts, inner)]
            tick()
        size *= 2

    k_raw = dk_ref[...]
    k_t = kf.T.astype(BF16)
    sub = lax.broadcasted_iota(jnp.int32, (16, DHD), 0)
    for h in range(2):
        alive_row = (pid_row == pid_before).astype(F32)
        alive_col = (pid_col == pid_before).astype(F32)
        growth_row = jnp.exp(cum[h : h + 1]) * alive_row
        growth_col = jnp.exp(packed[:, h : h + 1]) * alive_col
        beta_row = beta_ref[h : h + 1, :]
        u = dot2(split(inverses[h] * beta_row), dv_ref[:, h * DHD : (h + 1) * DHD])
        w = dot2(split(inverses[h] * (beta_row * growth_row * rk_row)), k_raw)
        wu = jnp.concatenate([w, u], axis=1)
        last = cum[h : h + 1, TOK - 1 : TOK]
        tail = jnp.where(pid_col == pid_last, jnp.exp(last - packed[:, h : h + 1]), 0.0) * rk_col
        tw = split(wu * tail)
        maps = dot(k_t, tw[0]) + dot(k_t, tw[1])
        gamma = jnp.broadcast_to(growth_row[:, TOK - 1 : TOK], (1, DHD))
        g_hi = gamma.astype(BF16).astype(F32)
        own[h, 0:DHD] = maps[:, :DHD]
        own[h, DHD : 2 * DHD] = maps[:, DHD:]
        own[h, 2 * DHD :] = jnp.where(sub == 0, g_hi, jnp.where(sub == 1, gamma - g_hi, 0.0))
        csend[0, h] = own[h].astype(BF16)
        pw = dot3(split(qk * decays[h]), split(wu))
        eff[h, :, :DHD] = (growth_col * rq_col) * qf - pw[:, :DHD]
        eff[h, :, DHD:] = pw[:, DHD:]
        tick()

    def chain_send(step, slot, distance):
        return copy(csend.at[step], crecv.at[slot], c_s.at[slot], c_r.at[slot], grp, ctx + distance)

    def chain_start(step, slot, distance):
        @pl.when(ctx + distance < 32)
        def _():
            chain_send(step, slot, distance).start()

    def chain_wait(slot, distance):
        @pl.when(ctx >= distance)
        def _():
            arrived(crecv.at[slot], c_r.at[slot])

        @pl.when(ctx < distance)
        def _():
            crecv[slot] = jnp.zeros((2, MSG, DHD), BF16)

    def unpack(message):
        gamma = jnp.sum(message[2 * DHD :].astype(F32), axis=0, keepdims=True)
        return message[0:DHD], message[DHD : 2 * DHD], gamma

    def compose(later, earlier, maps=True):
        g2, o2, y2 = later
        g1, o1, y1 = earlier
        if not maps:
            return None, y2 * o1.astype(F32) - dot(g2, o1) + o2.astype(F32), None
        both = dot(g2, jnp.concatenate([g1, o1], axis=1))
        g = y2 * g1.astype(F32) + y1 * g2.astype(F32) - both[:, :DHD]
        o = y2 * o1.astype(F32) - both[:, DHD:] + o2.astype(F32)
        return g, o, y2 * y1

    def pack(step, h, g, o, gamma):
        g_hi = gamma.astype(BF16).astype(F32)
        csend[step, h, 0:DHD] = g.astype(BF16)
        csend[step, h, DHD : 2 * DHD] = o.astype(BF16)
        csend[step, h, 2 * DHD :] = jnp.where(sub == 0, g_hi, jnp.where(sub == 1, gamma - g_hi, 0.0)).astype(BF16)

    chain_start(0, 0, 1)
    chain_start(0, 1, 2)

    acc[...] = jnp.zeros_like(acc)
    for hh in range(4):
        stat[hh, 0:1] = jnp.full((1, TOK), START_MAX, F32)
        stat[hh, 1:2] = jnp.zeros((1, TOK), F32)
    quad_ready = [False]

    def attend(dy):
        tick_through(dy)
        if not quad_ready[0]:
            quad_ready[0] = True
            for i in range(3):
                arrived(qall.at[quad_member[i]], q_r.at[i])

        @pl.when(y >= dy)
        def _():
            key_pos = ((y - dy) * 4 + col_i // PIECE) * TOK + member * PIECE + col_i % PIECE
            keep = (key_pos <= first + row_i) & (prompt(key_pos) == pid_row)
            bias[...] = jnp.where(keep, 0.0, MASKED)
            keys = kv[dy, 0].reshape(TOK, HD)
            vals_t = kv[dy, 1].reshape(TOK, HD).T

            def one(hh, carry):
                s = dot(keys, qall[hh], NT) + bias[...]
                old = stat[hh, 0:1]
                new = jnp.maximum(old, jnp.max(s, axis=0, keepdims=True))
                scale = jnp.exp(old - new)
                p = jnp.exp(s - new)
                stat[hh, 0:1] = new
                stat[hh, 1:2] = stat[hh, 1:2] * scale + jnp.sum(p, axis=0, keepdims=True)
                acc[hh] = acc[hh] * scale + dot(vals_t, p.astype(BF16))
                return carry

            lax.fori_loop(0, 4, one, 0)

    attend(0)
    chain_wait(0, 1)
    chain_wait(1, 2)
    for h in range(2):
        pack(1, h, *compose(unpack(crecv[0, h]), unpack(crecv[1, h])))
    chain_start(1, 2, 2)
    attend(1)
    chain_wait(2, 2)
    for h in range(2):
        pack(2, h, *compose(unpack(csend[1, h]), unpack(crecv[2, h])))
    chain_start(2, 3, 4)
    attend(2)
    chain_wait(3, 4)
    for h in range(2):
        pack(3, h, *compose(unpack(csend[2, h]), unpack(crecv[3, h])))
    chain_start(3, 4, 8)
    attend(3)
    attend(4)

    for i in (1, 2, 0):
        accs[i] = acc[quad_member[i]].astype(BF16)
        stats[i] = stat[quad_member[i]]
        copy(stats.at[i], statr.at[i], t_s.at[i], t_r.at[i], quad_grp[i], ctx).start()
        copy(accs.at[i], accr.at[i], a_s.at[i], a_r.at[i], quad_grp[i], ctx).start()

    def project(p, heads, w_ref, w_copy):
        w_copy.wait()
        for b in range(8):
            part = dot(heads, w_ref[:, b * 256 : (b + 1) * 256]).astype(BF16)
            pbuf[p, 0, b] = part[:, :DHD]
            pbuf[p, 1, b] = part[:, DHD:]
            i = p * 8 + b
            copy(pbuf.at[p, 1 - c, b], r1.at[p, b], s1_s.at[i], s1_r.at[i], sib_grp, ctx).start()

    def pair_sum(p, b):
        arrived(r1.at[p, b], s1_r.at[p * 8 + b])
        return pbuf[p, c, b].astype(F32) + r1[p, b].astype(F32)

    def across_x(p):
        for d in (2, 1, 3):
            xd = (x + d) % 4
            for e in range(2):
                s2[p, d - 1, e] = pair_sum(p, xd * 2 + e).astype(BF16)
            i = p * 3 + d - 1
            copy(s2.at[p, d - 1], r2.at[p, d - 1], s2_s.at[i], s2_r.at[i], x_grp[d - 1], ctx).start()

    def across_z(p):
        far = pair_sum(p, x * 2 + 1 - zh)
        near = pair_sum(p, x * 2 + zh)
        for d in (1, 3, 2):
            arrived(r2.at[p, d - 1], s2_r.at[p * 3 + d - 1])
            far += r2[p, d - 1, 1 - zh].astype(F32)
            near += r2[p, d - 1, zh].astype(F32)
        s3[p] = far.astype(BF16)
        copy(s3.at[p], r3.at[p], s3_s.at[p], s3_r.at[p], z_grp, ctx).start()
        return near

    def finish(p, near, o_ref):
        arrived(r3.at[p], s3_r.at[p])
        o_ref[...] = (near + r3[p].astype(F32)).astype(BF16)

    maxes, sums_, parts = [], [], []
    for i in range(3):
        arrived(statr.at[i], t_r.at[i])
    top = stat[member, 0:1]
    for i in range(3):
        top = jnp.maximum(top, statr[i, 0:1])
    scale = jnp.exp(stat[member, 0:1] - top)
    total = stat[member, 1:2] * scale
    mixed = acc[member] * scale
    for i in (0, 1, 2):
        arrived(accr.at[i], a_r.at[i])
        scale = jnp.exp(statr[i, 0:1] - top)
        total += statr[i, 1:2] * scale
        mixed += accr[i].astype(F32) * scale
    core_out = (mixed / total).T
    attn_heads = (core_out * jax.nn.sigmoid(agate_ref[...].astype(F32))).astype(BF16)
    project(0, attn_heads, wa_ref, wa_copy)

    chain_wait(4, 8)
    heads = []
    across_x(0)
    for h in range(2):
        _, state, _ = compose(unpack(csend[3, h]), unpack(crecv[4, h]), maps=False)
        core = dot3(split(eff[h, :, :DHD]), split(state)) + eff[h, :, DHD:]
        squares = jnp.mean(core * core, axis=1, keepdims=True)
        gate = dgate_ref[:, h * DHD : (h + 1) * DHD].astype(F32)
        normed = core * lax.rsqrt(squares + EPS) * gain_ref[...]
        heads.append((normed * gate * jax.nn.sigmoid(gate)).astype(BF16))
    project(1, jnp.concatenate(heads, axis=1), wd_ref, wd_copy)
    near_a = across_z(0)
    across_x(1)
    finish(0, near_a, oa_ref)
    near_d = across_z(1)
    finish(1, near_d, od_ref)

    for i in range(3):
        copy(kv.at[0, :, z], kv.at[0, :, z], z_s.at[i], kv_r.at[z], grp, row_ctx[i]).wait_send()
        copy(qall.at[member], qall.at[member], q_s.at[i], q_r.at[i], quad_grp[i], ctx).wait_send()
        copy(stats.at[i], statr.at[i], t_s.at[i], t_r.at[i], quad_grp[i], ctx).wait_send()
        copy(accs.at[i], accr.at[i], a_s.at[i], a_r.at[i], quad_grp[i], ctx).wait_send()
    for dy in range(4):

        @pl.when((y >= dy) & (y < 7))
        def _():
            for zs in range(4):
                forward(dy, zs).wait_send()

    for step, slot, distance in ((0, 0, 1), (0, 1, 2), (1, 2, 2), (2, 3, 4), (3, 4, 8)):

        @pl.when(ctx + distance < 32)
        def _():
            chain_send(step, slot, distance).wait_send()

    for p in range(2):
        for b in range(8):
            i = p * 8 + b
            copy(pbuf.at[p, 1 - c, b], r1.at[p, b], s1_s.at[i], s1_r.at[i], sib_grp, ctx).wait_send()
        for d in range(3):
            i = p * 3 + d
            copy(s2.at[p, d], r2.at[p, d], s2_s.at[i], s2_r.at[i], x_grp[d], ctx).wait_send()
        copy(s3.at[p], r3.at[p], s3_s.at[p], s3_r.at[p], z_grp, ctx).wait_send()


def local(
    queries,
    keys,
    values,
    attn_gate,
    delta_query,
    delta_key,
    delta_value,
    delta_gate,
    decay_log,
    beta,
    norm_gain,
    attn_out_weight,
    delta_out_weight,
    doc_lengths,
):
    ends = (jnp.cumsum(doc_lengths) * BLOCK).astype(jnp.int32)
    vmem = pl.BlockSpec(memory_space=pltpu.VMEM)
    anywhere = pl.BlockSpec(memory_space=pl.ANY)
    dma = lambda n: pltpu.SemaphoreType.DMA((n,))
    out = jax.ShapeDtypeStruct((TOK, DHD), BF16)
    return pl.pallas_call(
        kernel,
        out_shape=(out, out),
        in_specs=[pl.BlockSpec(memory_space=pltpu.SMEM)] + [vmem] * 11 + [anywhere] * 2,
        out_specs=(vmem, vmem),
        scratch_shapes=[
            pltpu.VMEM((256, 2048), BF16),
            pltpu.VMEM((256, 2048), BF16),
            pltpu.VMEM((4, TOK, HD), BF16),
            pltpu.VMEM((5, 2, 4, PIECE, HD), BF16),
            pltpu.VMEM((TOK, TOK), F32),
            pltpu.VMEM((4, HD, TOK), F32),
            pltpu.VMEM((4, 8, TOK), F32),
            pltpu.VMEM((3, HD, TOK), BF16),
            pltpu.VMEM((3, HD, TOK), BF16),
            pltpu.VMEM((3, 8, TOK), F32),
            pltpu.VMEM((3, 8, TOK), F32),
            pltpu.VMEM((2, MSG, DHD), F32),
            pltpu.VMEM((4, 2, MSG, DHD), BF16),
            pltpu.VMEM((5, 2, MSG, DHD), BF16),
            pltpu.VMEM((2, TOK, 2 * DHD), F32),
            pltpu.VMEM((2, 2, 8, TOK, DHD), BF16),
            pltpu.VMEM((2, 8, TOK, DHD), BF16),
            pltpu.VMEM((2, 3, 2, TOK, DHD), BF16),
            pltpu.VMEM((2, 3, 2, TOK, DHD), BF16),
            pltpu.VMEM((2, TOK, DHD), BF16),
            pltpu.VMEM((2, TOK, DHD), BF16),
            dma(2),
            dma(3),
            dma(3),
            dma(3),
            dma(16),
            dma(20),
            dma(5),
            dma(5),
            dma(3),
            dma(3),
            dma(3),
            dma(3),
            dma(16),
            dma(16),
            dma(6),
            dma(6),
            dma(2),
            dma(2),
        ],
        compiler_params=pltpu.CompilerParams(
            collective_id=0, has_side_effects=True, vmem_limit_bytes=48 * 1024 * 1024
        ),
        cost_estimate=pl.CostEstimate(flops=4 * 10**9, bytes_accessed=6 * 10**6, transcendentals=2 * 10**6),
    )(
        ends,
        queries,
        keys,
        values,
        attn_gate,
        delta_query,
        delta_key,
        delta_value,
        delta_gate,
        decay_log,
        beta,
        norm_gain.reshape(1, DHD),
        attn_out_weight,
        delta_out_weight,
    )


def solution(mesh):
    placed = (
        P("ctx", "grp"),
        P("ctx", None),
        P("ctx", None),
        P("ctx", "grp"),
        P("ctx", "grp"),
        P("ctx", "grp"),
        P("ctx", "grp"),
        P("ctx", "grp"),
        P("grp", "ctx"),
        P("grp", "ctx"),
        P(),
        P("grp", None),
        P("grp", None),
        P(),
    )
    return jax.shard_map(
        local,
        mesh=mesh,
        in_specs=placed,
        out_specs=(P("ctx", "grp"), P("ctx", "grp")),
        check_vma=False,
    )
```

time: 977 us -> 110 us (0.11)
  the two profiles are of different devices: /device:TPU:56 before, /device:TPU:240 now
where the time goes in v1:
time: 110 us; the launch traced here: 109 us
  Pallas kernels  96.2 us (87%)
  local copies, waits for them, and re-layouts  12.2 us (11%)
    pallas_call x1, Pallas kernels, local(): pl.pallas_call(kernel, out_shape=(out, out), in_specs=[pl.BlockSpec(memor...  96.2 us
    unnamed x30, local copies, waits for them, and re-layouts  12.2 us

profile of v1, /device:TPU:240, one launch (start us, length us, event | category | flops | bytes accessed | tf_op | source)
XLA Modules:
  0.0 109.2 jit_solution(9694575961007945026)
XLA Ops:
  0.6 0.0 copy-start.13
  0.6 0.0 copy-start.11
  0.7 0.6 copy-done.13
  1.3 0.0 copy-start.10
  1.3 0.2 reduce-window.9
  1.5 0.0 copy-start.12
  1.5 0.0 copy-done.11
  1.5 0.5 copy-done.10
  2.0 0.2 copy-done.12
  2.1 0.0 copy-start
  2.1 1.2 %copy-done = bf16[256,2048]{1,0:T(8,128)(2,1)S(1)} copy-done((bf16[256,2048]{1,0:T(8,128)(2,1)S(1)}, bf16[256,2048]{1,0:T(8,128)(2,1)}, u32[]{:S(2)}) %copy-start) | copy-done | bytes 1048600
  3.3 0.0 copy-start.1
  3.3 1.2 %copy-done.1 = bf16[256,2048]{1,0:T(8,128)(2,1)S(1)} copy-done((bf16[256,2048]{1,0:T(8,128)(2,1)S(1)}, bf16[256,2048]{1,0:T(8,128)(2,1)}, u32[]{:S(2)}) %copy-start.1) | copy-done | bytes 1048600
  4.6 0.0 copy-start.2
  4.6 0.9 copy-done.2
  5.5 0.0 copy-start.3
  5.5 0.9 copy-done.3
  6.5 0.0 copy-start.4
  6.5 0.9 copy-done.4
  7.4 0.0 copy-start.5
  7.4 0.9 copy-done.5
  8.3 0.0 copy-start.6
  8.3 0.9 copy-done.6
  9.2 0.0 copy-start.7
  9.2 0.9 copy-done.7
  10.1 0.0 copy-start.8
  10.1 0.8 copy-done.8
  10.9 0.0 copy-start.9
  10.9 0.8 copy-done.9
  11.8 96.2 %shard_map.149 = (bf16[256,128]{1,0:T(8,128)(2,1)S(1)}, bf16[256,128]{1,0:T(8,128)(2,1)S(1)}) custom-call(s32[4]{0:T(128)S(1)} %multiply_bitcast_fusion.ends_ref, bf16[256,256]{1,0:T(8,128)(2,1)S(1)} %copy-done.4, bf16[256,512]{1,0:T(8,128)(2,1)S(1)} %copy-done.2, bf16[256,512]{1,0:T(8,128)(2,1)S(1)} %copy-done.3, bf16[256,256]{1,0:T(8,128)(2,1)S(1)} %copy-done.5, ...), custom_call_target="tpu_custom_call" | custom-call | flops 4000000000 | bytes 6000000 | tf_op jit(solution)/shard_map/pallas_call | solution.py:507
  108.0 0.6 copy.18
  108.6 0.6 copy.19
  (1 shorter events, 0.0 us)
Async XLA Ops:
  0.6 0.7 copy-start.13
  0.6 0.8 copy-start.11
  1.3 0.7 copy-start.10
  1.5 0.7 copy-start.12
  2.1 1.2 %copy-start = (bf16[256,2048]{1,0:T(8,128)(2,1)S(1)}, bf16[256,2048]{1,0:T(8,128)(2,1)}, u32[]{:S(2)}) copy-start(bf16[256,2048]{1,0:T(8,128)(2,1)} %wa_hbm.1) | copy-start | bytes 3145732
  3.3 1.2 %copy-start.1 = (bf16[256,2048]{1,0:T(8,128)(2,1)S(1)}, bf16[256,2048]{1,0:T(8,128)(2,1)}, u32[]{:S(2)}) copy-start(bf16[256,2048]{1,0:T(8,128)(2,1)} %wd_hbm.1) | copy-start | bytes 3145732
  4.6 0.9 copy-start.2
  5.5 0.9 copy-start.3
  6.5 0.9 copy-start.4
  7.4 0.9 copy-start.5
  8.3 0.9 copy-start.6
  9.2 0.9 copy-start.7
  10.1 0.8 copy-start.8
  10.9 0.8 copy-start.9

commit v2 on v1

--- a/solution.py
+++ b/solution.py
@@ -48,10 +48,23 @@
 
 
 def kernel(
-    ends_ref,
+    lengths_ref,
+    q_hbm,
+    k_hbm,
+    v_hbm,
+    agate_hbm,
+    dq_hbm,
+    dk_hbm,
+    dv_hbm,
+    dgate_hbm,
+    decay_hbm,
+    beta_hbm,
+    gain_hbm,
+    wa_hbm,
+    wd_hbm,
+    oa_ref,
+    od_ref,
     q_ref,
-    k_ref,
-    v_ref,
     agate_ref,
     dq_ref,
     dk_ref,
@@ -60,10 +73,6 @@
     decay_ref,
     beta_ref,
     gain_ref,
-    wa_hbm,
-    wd_hbm,
-    oa_ref,
-    od_ref,
     wa_ref,
     wd_ref,
     qall,
@@ -146,15 +155,32 @@
     for g, r in peers:
         pl.semaphore_signal(barrier, inc=1, device_id={"grp": g, "ctx": r}, device_id_type=MESH)
 
-    wa_copy = pltpu.make_async_copy(wa_hbm, wa_ref, w_sem.at[0])
-    wd_copy = pltpu.make_async_copy(wd_hbm, wd_ref, w_sem.at[1])
-    wa_copy.start()
-    wd_copy.start()
-
     rows = pl.ds(pl.multiple_of(member * PIECE, PIECE), PIECE)
     cols = pl.ds(pl.multiple_of(kvh * HD, HD), HD)
-    kv[0, 0, z] = k_ref[rows, cols]
-    kv[0, 1, z] = v_ref[rows, cols]
+    loads = [
+        pltpu.make_async_copy(src, dst, w_sem.at[i])
+        for i, (src, dst) in enumerate(
+            [
+                (k_hbm.at[rows, cols], kv.at[0, 0, z]),
+                (v_hbm.at[rows, cols], kv.at[0, 1, z]),
+                (q_hbm, q_ref),
+                (dk_hbm, dk_ref),
+                (dq_hbm, dq_ref),
+                (decay_hbm, decay_ref),
+                (beta_hbm, beta_ref),
+                (dv_hbm, dv_ref),
+                (gain_hbm, gain_ref),
+                (dgate_hbm, dgate_ref),
+                (agate_hbm, agate_ref),
+                (wd_hbm, wd_ref),
+                (wa_hbm, wa_ref),
+            ]
+        )
+    ]
+    for load in loads:
+        load.start()
+    for load in loads[:3]:
+        load.wait()
     qall[member] = q_ref[...] * jnp.asarray(HD ** (-0.5), BF16)
     pl.semaphore_wait(barrier, len(peers))
 
@@ -172,7 +198,8 @@
     for i in (1, 2, 0):
         copy(qall.at[member], qall.at[member], q_s.at[i], q_r.at[i], quad_grp[i], ctx).start()
 
-    ticks = [(dy, i) for dy in range(5) for i in range(4)][1:]
+    ticks = [(1, 0), (0, 1), (0, 2), (0, 3), (2, 0), (1, 1), (1, 2), (1, 3), (3, 0), (2, 1)]
+    ticks += [(2, 2), (2, 3), (4, 0), (3, 1), (3, 2), (3, 3), (4, 1), (4, 2), (4, 3)]
 
     def tick(count=1):
         for _ in range(count):
@@ -192,11 +219,15 @@
                         forward(dy, zs).start()
 
     def tick_through(dy):
-        while ticks and ticks[0][0] <= dy:
+        while any(t[0] <= dy for t in ticks):
             tick()
 
     first = ctx * TOK
-    ends = [ends_ref[i] for i in range(4)]
+    ends = [lengths_ref[0] * BLOCK]
+    for i in range(1, 4):
+        ends.append(ends[-1] + lengths_ref[i] * BLOCK)
+    for load in loads[3:9]:
+        load.wait()
 
     def prompt(pos):
         total = (pos >= ends[0]).astype(F32)
@@ -234,7 +265,6 @@
     packed = jnp.concatenate([cum, beta_ref[...], jnp.zeros((DHD - 4, TOK), F32)], axis=0).T
     kk = dot(dk_ref[...], dk_ref[...], NT) * rk_col * rk_row
     qk = dot(dq_ref[...], dk_ref[...], NT) * rq_col * rk_row
-    tick()
 
     decays, lows = [], []
     for h in range(2):
@@ -242,7 +272,6 @@
         decay = jnp.where(lower, jnp.exp(jnp.where(lower, diff, 0.0)), 0.0)
         decays.append(decay)
         lows.append(jnp.where(strict, packed[:, 2 + h : 3 + h] * decay * kk, 0.0))
-    tick()
 
     eye = (ii == jj).astype(F32)
     inverses = None
@@ -255,7 +284,8 @@
             parts = [split(t) for t in inverses]
             inner = [dot3(split(jnp.where(cross, low, 0.0)), t) for low, t in zip(lows, parts)]
             inverses = [t - dot3(tp, split(m)) for t, tp, m in zip(inverses, parts, inner)]
-            tick()
+            if size >= 32:
+                tick()
         size *= 2
 
     k_raw = dk_ref[...]
@@ -283,10 +313,11 @@
         pw = dot3(split(qk * decays[h]), split(wu))
         eff[h, :, :DHD] = (growth_col * rq_col) * qf - pw[:, :DHD]
         eff[h, :, DHD:] = pw[:, DHD:]
-        tick()
 
     def chain_send(step, slot, distance):
-        return copy(csend.at[step], crecv.at[slot], c_s.at[slot], c_r.at[slot], grp, ctx + distance)
+        part = pl.ds(0, MSG) if distance < 8 else pl.ds(DHD, DHD)
+        src, dst = csend.at[step, :, part], crecv.at[slot, :, part]
+        return copy(src, dst, c_s.at[slot], c_r.at[slot], grp, ctx + distance)
 
     def chain_start(step, slot, distance):
         @pl.when(ctx + distance < 32)
@@ -296,7 +327,8 @@
     def chain_wait(slot, distance):
         @pl.when(ctx >= distance)
         def _():
-            arrived(crecv.at[slot], c_r.at[slot])
+            part = pl.ds(0, MSG) if distance < 8 else pl.ds(DHD, DHD)
+            arrived(crecv.at[slot, :, part], c_r.at[slot])
 
         @pl.when(ctx < distance)
         def _():
@@ -306,11 +338,13 @@
         gamma = jnp.sum(message[2 * DHD :].astype(F32), axis=0, keepdims=True)
         return message[0:DHD], message[DHD : 2 * DHD], gamma
 
-    def compose(later, earlier, maps=True):
+    def apply_map(later, o1):
+        g2, o2, y2 = later
+        return y2 * o1.astype(F32) - dot(g2, o1) + o2.astype(F32)
+
+    def compose(later, earlier):
         g2, o2, y2 = later
         g1, o1, y1 = earlier
-        if not maps:
-            return None, y2 * o1.astype(F32) - dot(g2, o1) + o2.astype(F32), None
         both = dot(g2, jnp.concatenate([g1, o1], axis=1))
         g = y2 * g1.astype(F32) + y1 * g2.astype(F32) - both[:, :DHD]
         o = y2 * o1.astype(F32) - both[:, DHD:] + o2.astype(F32)
@@ -331,33 +365,39 @@
         stat[hh, 1:2] = jnp.zeros((1, TOK), F32)
     quad_ready = [False]
 
-    def attend(dy):
+    heads_order = [quad_member[1], quad_member[2], quad_member[0], member]
+
+    def attend(dy, then=None):
         tick_through(dy)
         if not quad_ready[0]:
             quad_ready[0] = True
             for i in range(3):
                 arrived(qall.at[quad_member[i]], q_r.at[i])
 
-        @pl.when(y >= dy)
-        def _():
+        def masks():
             key_pos = ((y - dy) * 4 + col_i // PIECE) * TOK + member * PIECE + col_i % PIECE
             keep = (key_pos <= first + row_i) & (prompt(key_pos) == pid_row)
             bias[...] = jnp.where(keep, 0.0, MASKED)
+
+        def one(hh):
             keys = kv[dy, 0].reshape(TOK, HD)
+            s = dot(keys, qall[hh], NT) + bias[...]
+            old = stat[hh, 0:1]
+            new = jnp.maximum(old, jnp.max(s, axis=0, keepdims=True))
+            scale = jnp.exp(old - new)
+            p = jnp.exp(s - new)
+            stat[hh, 0:1] = new
+            stat[hh, 1:2] = stat[hh, 1:2] * scale + jnp.sum(p, axis=0, keepdims=True)
             vals_t = kv[dy, 1].reshape(TOK, HD).T
-
-            def one(hh, carry):
-                s = dot(keys, qall[hh], NT) + bias[...]
-                old = stat[hh, 0:1]
-                new = jnp.maximum(old, jnp.max(s, axis=0, keepdims=True))
-                scale = jnp.exp(old - new)
-                p = jnp.exp(s - new)
-                stat[hh, 0:1] = new
-                stat[hh, 1:2] = stat[hh, 1:2] * scale + jnp.sum(p, axis=0, keepdims=True)
-                acc[hh] = acc[hh] * scale + dot(vals_t, p.astype(BF16))
-                return carry
-
-            lax.fori_loop(0, 4, one, 0)
+            acc[hh] = acc[hh] * scale + dot(vals_t, p.astype(BF16))
+
+        pl.when(y >= dy)(masks)
+        for n, hh in enumerate(heads_order):
+            pl.when(y >= dy)(functools.partial(one, hh))
+            if then is not None:
+                then(n)
+            else:
+                tick()
 
     attend(0)
     chain_wait(0, 1)
@@ -376,16 +416,8 @@
         pack(3, h, *compose(unpack(csend[2, h]), unpack(crecv[3, h])))
     chain_start(3, 4, 8)
     attend(3)
-    attend(4)
-
-    for i in (1, 2, 0):
-        accs[i] = acc[quad_member[i]].astype(BF16)
-        stats[i] = stat[quad_member[i]]
-        copy(stats.at[i], statr.at[i], t_s.at[i], t_r.at[i], quad_grp[i], ctx).start()
-        copy(accs.at[i], accr.at[i], a_s.at[i], a_r.at[i], quad_grp[i], ctx).start()
-
-    def project(p, heads, w_ref, w_copy):
-        w_copy.wait()
+
+    def project(p, heads, w_ref):
         for b in range(8):
             part = dot(heads, w_ref[:, b * 256 : (b + 1) * 256]).astype(BF16)
             pbuf[p, 0, b] = part[:, :DHD]
@@ -420,7 +452,33 @@
         arrived(r3.at[p], s3_r.at[p])
         o_ref[...] = (near + r3[p].astype(F32)).astype(BF16)
 
-    maxes, sums_, parts = [], [], []
+    for load in (loads[9], loads[11]):
+        load.wait()
+    chain_wait(4, 8)
+    heads = []
+    for h in range(2):
+        state = apply_map(unpack(csend[3, h]), crecv[4, h, DHD : 2 * DHD])
+        core = dot3(split(eff[h, :, :DHD]), split(state)) + eff[h, :, DHD:]
+        squares = jnp.mean(core * core, axis=1, keepdims=True)
+        gate = dgate_ref[:, h * DHD : (h + 1) * DHD].astype(F32)
+        normed = core * lax.rsqrt(squares + EPS) * gain_ref[...]
+        heads.append((normed * gate * jax.nn.sigmoid(gate)).astype(BF16))
+    project(1, jnp.concatenate(heads, axis=1), wd_ref)
+    tick(4)
+
+    def send_partial(n):
+        if n == 3:
+            return
+        i = (1, 2, 0)[n]
+        accs[i] = acc[quad_member[i]].astype(BF16)
+        stats[i] = stat[quad_member[i]]
+        copy(stats.at[i], statr.at[i], t_s.at[i], t_r.at[i], quad_grp[i], ctx).start()
+        copy(accs.at[i], accr.at[i], a_s.at[i], a_r.at[i], quad_grp[i], ctx).start()
+
+    attend(4, send_partial)
+    across_x(1)
+    for load in (loads[10], loads[12]):
+        load.wait()
     for i in range(3):
         arrived(statr.at[i], t_r.at[i])
     top = stat[member, 0:1]
@@ -436,24 +494,12 @@
         mixed += accr[i].astype(F32) * scale
     core_out = (mixed / total).T
     attn_heads = (core_out * jax.nn.sigmoid(agate_ref[...].astype(F32))).astype(BF16)
-    project(0, attn_heads, wa_ref, wa_copy)
-
-    chain_wait(4, 8)
-    heads = []
+    project(0, attn_heads, wa_ref)
+    near_d = across_z(1)
     across_x(0)
-    for h in range(2):
-        _, state, _ = compose(unpack(csend[3, h]), unpack(crecv[4, h]), maps=False)
-        core = dot3(split(eff[h, :, :DHD]), split(state)) + eff[h, :, DHD:]
-        squares = jnp.mean(core * core, axis=1, keepdims=True)
-        gate = dgate_ref[:, h * DHD : (h + 1) * DHD].astype(F32)
-        normed = core * lax.rsqrt(squares + EPS) * gain_ref[...]
-        heads.append((normed * gate * jax.nn.sigmoid(gate)).astype(BF16))
-    project(1, jnp.concatenate(heads, axis=1), wd_ref, wd_copy)
+    finish(1, near_d, od_ref)
     near_a = across_z(0)
-    across_x(1)
     finish(0, near_a, oa_ref)
-    near_d = across_z(1)
-    finish(1, near_d, od_ref)
 
     for i in range(3):
         copy(kv.at[0, :, z], kv.at[0, :, z], z_s.at[i], kv_r.at[z], grp, row_ctx[i]).wait_send()
@@ -499,17 +545,25 @@
     delta_out_weight,
     doc_lengths,
 ):
-    ends = (jnp.cumsum(doc_lengths) * BLOCK).astype(jnp.int32)
     vmem = pl.BlockSpec(memory_space=pltpu.VMEM)
-    anywhere = pl.BlockSpec(memory_space=pl.ANY)
+    anywhere = pl.BlockSpec(memory_space=pltpu.HBM)
     dma = lambda n: pltpu.SemaphoreType.DMA((n,))
     out = jax.ShapeDtypeStruct((TOK, DHD), BF16)
     return pl.pallas_call(
         kernel,
         out_shape=(out, out),
-        in_specs=[pl.BlockSpec(memory_space=pltpu.SMEM)] + [vmem] * 11 + [anywhere] * 2,
+        in_specs=[pl.BlockSpec(memory_space=pltpu.SMEM)] + [anywhere] * 13,
         out_specs=(vmem, vmem),
         scratch_shapes=[
+            pltpu.VMEM((TOK, HD), BF16),
+            pltpu.VMEM((TOK, HD), BF16),
+            pltpu.VMEM((TOK, DHD), BF16),
+            pltpu.VMEM((TOK, DHD), BF16),
+            pltpu.VMEM((TOK, 2 * DHD), BF16),
+            pltpu.VMEM((TOK, 2 * DHD), BF16),
+            pltpu.VMEM((2, TOK), F32),
+            pltpu.VMEM((2, TOK), F32),
+            pltpu.VMEM((1, DHD), F32),
             pltpu.VMEM((256, 2048), BF16),
             pltpu.VMEM((256, 2048), BF16),
             pltpu.VMEM((4, TOK, HD), BF16),
@@ -531,7 +585,7 @@
             pltpu.VMEM((2, 3, 2, TOK, DHD), BF16),
             pltpu.VMEM((2, TOK, DHD), BF16),
             pltpu.VMEM((2, TOK, DHD), BF16),
-            dma(2),
+            dma(13),
             dma(3),
             dma(3),
             dma(3),
@@ -551,11 +605,11 @@
             dma(2),
         ],
         compiler_params=pltpu.CompilerParams(
-            collective_id=0, has_side_effects=True, vmem_limit_bytes=48 * 1024 * 1024
+            collective_id=0, has_side_effects=True, vmem_limit_bytes=64 * 1024 * 1024
         ),
         cost_estimate=pl.CostEstimate(flops=4 * 10**9, bytes_accessed=6 * 10**6, transcendentals=2 * 10**6),
     )(
-        ends,
+        doc_lengths,
         queries,
         keys,
         values,

time: 110 us -> 83.6 us (0.76)
  the two profiles are of different devices: /device:TPU:240 before, /device:TPU:104 now
where the time goes in v2:
time: 83.6 us; the launch traced here: 83.4 us
  Pallas kernels  80.6 us (96%)
  local copies, waits for them, and re-layouts  2.14 us (3%)
    pallas_call x1, Pallas kernels, local(): pl.pallas_call(kernel, out_shape=(out, out), in_specs=[pl.BlockSpec(memor...  80.6 us
    unnamed x4, local copies, waits for them, and re-layouts  2.14 us

profile of v2, /device:TPU:104, one launch (start us, length us, event | category | flops | bytes accessed | tf_op | source)
XLA Modules:
  0.0 83.4 jit_solution(13804265553445552071)
XLA Ops:
  0.6 80.6 %shard_map.149 = (bf16[256,128]{1,0:T(8,128)(2,1)}, bf16[256,128]{1,0:T(8,128)(2,1)}) custom-call(s32[4]{0:T(128)} %lengths_ref.1, bf16[256,256]{1,0:T(8,128)(2,1)} %q_hbm.1, bf16[256,512]{1,0:T(8,128)(2,1)} %k_hbm.1, bf16[256,512]{1,0:T(8,128)(2,1)} %v_hbm.1, bf16[256,256]{1,0:T(8,128)(2,1)} %agate_hbm.1, bf16[256,128]{1,0:T(8,128)(2,1)} %dq_hbm.1, ...), custom_call_target="tpu_custom_call" | custom-call | flops 4000000000 | bytes 6000000 | tf_op jit(solution)/shard_map/pallas_call | solution.py:552
  81.2 0.0 copy-start
  81.2 1.5 %copy.18 = bf16[256,128]{1,0:T(8,128)(2,1)} copy(bf16[256,128]{1,0:T(8,128)(2,1)} %get-tuple-element.4) | data formatting | bytes 131072
  82.8 0.0 copy-done
  82.8 0.6 copy.19
Async XLA Ops:
  81.2 1.5 %copy-start = (bf16[256,128]{1,0:T(8,128)(2,1)S(1)}, bf16[256,128]{1,0:T(8,128)(2,1)}, u32[]{:S(2)}) copy-start(bf16[256,128]{1,0:T(8,128)(2,1)} %get-tuple-element.5) | copy-start | bytes 196612

commit v3 on v2

--- a/solution.py
+++ b/solution.py
@@ -18,6 +18,7 @@
 BLOCK = 64
 TOK = 256
 PIECE = 64
+QUARTER = DHD // 4
 MSG = 2 * DHD + 16
 
 EPS = 1e-06
@@ -77,21 +78,25 @@
     wd_ref,
     qall,
     kv,
-    bias,
     acc,
     stat,
     accs,
     accr,
     stats,
     statr,
-    own,
     csend,
     crecv,
+    tsend,
+    trecv,
+    tall,
+    state,
     eff,
     pbuf,
     r1,
     s2,
     r2,
+    s4,
+    r4,
     s3,
     r3,
     w_sem,
@@ -102,6 +107,10 @@
     kv_r,
     c_s,
     c_r,
+    h_s,
+    h_r,
+    g_s,
+    g_r,
     a_s,
     a_r,
     t_s,
@@ -128,9 +137,11 @@
     quad = [(x, 1 - c), (xn, c), (xn, 1 - c)]
     quad_grp = [grp_of(a, zh, b) for a, b in quad]
     quad_member = [(a % 2) * 2 + b for a, b in quad]
-    x_grp = [grp_of((x + d) % 4, zh, c) for d in (1, 2, 3)]
     z_grp = grp_of(x, 1 - zh, c)
-    sib_grp = quad_grp[0]
+    sib_grp, xn_grp = quad_grp[0], quad_grp[1]
+    xm = (x + 3 + 2 * xb) % 4
+    xo = (x + 2) % 4
+    xm_grp = grp_of(xm, zh, c)
     row_ctx = [y * 4 + (z + d) % 4 for d in (1, 2, 3)]
 
     def copy(src, dst, send, recv, g, r):
@@ -149,9 +160,9 @@
     sends = []
 
     barrier = pltpu.get_barrier_semaphore()
-    peers = [(g, ctx) for g in quad_grp + x_grp + [z_grp]]
+    peers = [(g, ctx) for g in quad_grp + [xm_grp, z_grp]]
     peers += [(grp, r) for r in row_ctx]
-    peers += [(grp, (ctx + d) % 32) for d in (1, 31, 2, 30, 4, 28, 8, 24)]
+    peers += [(grp, (ctx + d) % 32) for d in (4, 28)]
     for g, r in peers:
         pl.semaphore_signal(barrier, inc=1, device_id={"grp": g, "ctx": r}, device_id_type=MESH)
 
@@ -198,8 +209,7 @@
     for i in (1, 2, 0):
         copy(qall.at[member], qall.at[member], q_s.at[i], q_r.at[i], quad_grp[i], ctx).start()
 
-    ticks = [(1, 0), (0, 1), (0, 2), (0, 3), (2, 0), (1, 1), (1, 2), (1, 3), (3, 0), (2, 1)]
-    ticks += [(2, 2), (2, 3), (4, 0), (3, 1), (3, 2), (3, 3), (4, 1), (4, 2), (4, 3)]
+    ticks = [(1, 0), (0, 1), (0, 2), (0, 3)] + [(dy, i) for dy in range(1, 5) for i in range(4)][1:]
 
     def tick(count=1):
         for _ in range(count):
@@ -284,13 +294,34 @@
             parts = [split(t) for t in inverses]
             inner = [dot3(split(jnp.where(cross, low, 0.0)), t) for low, t in zip(lows, parts)]
             inverses = [t - dot3(tp, split(m)) for t, tp, m in zip(inverses, parts, inner)]
-            if size >= 32:
+            if size == 128:
                 tick()
         size *= 2
+
+    def unpack(message):
+        gamma = jnp.sum(message[2 * DHD :].astype(F32), axis=0, keepdims=True)
+        return message[0:DHD], message[DHD : 2 * DHD], gamma
+
+    def apply_map(full, state_t, offset_t):
+        g, _, gamma = full
+        return gamma * state_t.astype(F32) - dot(state_t, g, NT) + offset_t.astype(F32)
+
+    def compose(after, before):
+        g2, o2, y2 = after
+        g1, o1, y1 = before
+        g = y2 * g1.astype(F32) + y1 * g2.astype(F32) - dot(g2, g1)
+        return g, apply_map(after, o1, o2), y2 * y1
+
+    def pack(step, h, g, o, gamma):
+        g_hi = gamma.astype(BF16).astype(F32)
+        csend[step, h, 0:DHD] = g.astype(BF16)
+        csend[step, h, DHD : 2 * DHD] = o.astype(BF16)
+        csend[step, h, 2 * DHD :] = jnp.where(sub == 0, g_hi, jnp.where(sub == 1, gamma - g_hi, 0.0)).astype(BF16)
 
     k_raw = dk_ref[...]
     k_t = kf.T.astype(BF16)
     sub = lax.broadcasted_iota(jnp.int32, (16, DHD), 0)
+    later = []
     for h in range(2):
         alive_row = (pid_row == pid_before).astype(F32)
         alive_col = (pid_col == pid_before).astype(F32)
@@ -302,120 +333,157 @@
         wu = jnp.concatenate([w, u], axis=1)
         last = cum[h : h + 1, TOK - 1 : TOK]
         tail = jnp.where(pid_col == pid_last, jnp.exp(last - packed[:, h : h + 1]), 0.0) * rk_col
-        tw = split(wu * tail)
+        tw = split(w * tail)
         maps = dot(k_t, tw[0]) + dot(k_t, tw[1])
+        offsets_t = dot2(split((u * tail).T), k_raw)
         gamma = jnp.broadcast_to(growth_row[:, TOK - 1 : TOK], (1, DHD))
-        g_hi = gamma.astype(BF16).astype(F32)
-        own[h, 0:DHD] = maps[:, :DHD]
-        own[h, DHD : 2 * DHD] = maps[:, DHD:]
-        own[h, 2 * DHD :] = jnp.where(sub == 0, g_hi, jnp.where(sub == 1, gamma - g_hi, 0.0))
-        csend[0, h] = own[h].astype(BF16)
+        pack(0, h, maps, offsets_t, gamma)
+        later.append((wu, growth_col))
+
+    def z_exchange(step):
+        peer = y * 4 + (z + 1 - 2 * (z % 2) if step == 0 else (z + 2) % 4)
+        return copy(csend.at[step], crecv.at[step], c_s.at[step], c_r.at[step], grp, peer)
+
+    z_exchange(0).start()
+    for h, (wu, growth_col) in enumerate(later):
+        tick()
         pw = dot3(split(qk * decays[h]), split(wu))
         eff[h, :, :DHD] = (growth_col * rq_col) * qf - pw[:, :DHD]
         eff[h, :, DHD:] = pw[:, DHD:]
 
-    def chain_send(step, slot, distance):
-        part = pl.ds(0, MSG) if distance < 8 else pl.ds(DHD, DHD)
-        src, dst = csend.at[step, :, part], crecv.at[slot, :, part]
-        return copy(src, dst, c_s.at[slot], c_r.at[slot], grp, ctx + distance)
-
-    def chain_start(step, slot, distance):
-        @pl.when(ctx + distance < 32)
+    def fold(step, recv_is_later):
+        arrived(crecv.at[step], c_r.at[step])
+        for first_later in (True, False):
+
+            @pl.when(recv_is_later if first_later else jnp.logical_not(recv_is_later))
+            def _():
+                for h in range(2):
+                    pair = unpack(crecv[step, h]), unpack(csend[step, h])
+                    pack(step + 1, h, *compose(*(pair if first_later else pair[::-1])))
+
+    quarter = pl.ds(pl.multiple_of(z * QUARTER, QUARTER), QUARTER)
+
+    def row_hop(k):
+        return copy(tsend.at[k], trecv.at[k], h_s.at[k], h_r.at[k], grp, ctx + 4)
+
+    def hop_start(k):
+        @pl.when(y < 7)
         def _():
-            chain_send(step, slot, distance).start()
-
-    def chain_wait(slot, distance):
-        @pl.when(ctx >= distance)
+            for h in range(2):
+                offset = csend[2, h, pl.ds(pl.multiple_of(DHD + z * QUARTER, QUARTER), QUARTER)]
+                if k == 0:
+                    tsend[k, h] = offset
+                else:
+                    tsend[k, h] = apply_map(unpack(csend[2, h]), trecv[k - 1, h], offset).astype(BF16)
+            row_hop(k).start()
+
+    def hop_wait(k):
+        @pl.when(y >= 1)
         def _():
-            part = pl.ds(0, MSG) if distance < 8 else pl.ds(DHD, DHD)
-            arrived(crecv.at[slot, :, part], c_r.at[slot])
-
-        @pl.when(ctx < distance)
+            arrived(trecv.at[k], h_r.at[k])
+
+        if k < 3:
+
+            @pl.when(y < 1)
+            def _():
+                trecv[k] = jnp.zeros((2, QUARTER, DHD), BF16)
+
+    def share(d):
+        part = tall.at[:, quarter]
+        return copy(part, part, g_s.at[d], g_r.at[d], grp, row_ctx[d])
+
+    def share_start():
+        @pl.when(y >= 1)
         def _():
-            crecv[slot] = jnp.zeros((2, MSG, DHD), BF16)
-
-    def unpack(message):
-        gamma = jnp.sum(message[2 * DHD :].astype(F32), axis=0, keepdims=True)
-        return message[0:DHD], message[DHD : 2 * DHD], gamma
-
-    def apply_map(later, o1):
-        g2, o2, y2 = later
-        return y2 * o1.astype(F32) - dot(g2, o1) + o2.astype(F32)
-
-    def compose(later, earlier):
-        g2, o2, y2 = later
-        g1, o1, y1 = earlier
-        both = dot(g2, jnp.concatenate([g1, o1], axis=1))
-        g = y2 * g1.astype(F32) + y1 * g2.astype(F32) - both[:, :DHD]
-        o = y2 * o1.astype(F32) - both[:, DHD:] + o2.astype(F32)
-        return g, o, y2 * y1
-
-    def pack(step, h, g, o, gamma):
-        g_hi = gamma.astype(BF16).astype(F32)
-        csend[step, h, 0:DHD] = g.astype(BF16)
-        csend[step, h, DHD : 2 * DHD] = o.astype(BF16)
-        csend[step, h, 2 * DHD :] = jnp.where(sub == 0, g_hi, jnp.where(sub == 1, gamma - g_hi, 0.0)).astype(BF16)
-
-    chain_start(0, 0, 1)
-    chain_start(0, 1, 2)
-
-    acc[...] = jnp.zeros_like(acc)
-    for hh in range(4):
-        stat[hh, 0:1] = jnp.full((1, TOK), START_MAX, F32)
-        stat[hh, 1:2] = jnp.zeros((1, TOK), F32)
+            tall[:, quarter] = trecv[3]
+
+        @pl.when(y < 1)
+        def _():
+            tall[:, quarter] = jnp.zeros((2, QUARTER, DHD), BF16)
+
+        for d in range(3):
+            share(d).start()
+
+    def share_wait():
+        for d in range(3):
+            theirs = pl.ds(pl.multiple_of((z + 3 - d) % 4 * QUARTER, QUARTER), QUARTER)
+            arrived(tall.at[:, theirs], g_r.at[d])
+        state[...] = tall[...]
+        for step, wanted in ((1, z >= 2), (0, z % 2 == 1)):
+
+            @pl.when(wanted)
+            def _():
+                for h in range(2):
+                    full = unpack(crecv[step, h])
+                    state[h] = apply_map(full, state[h], full[1]).astype(BF16)
+
     quad_ready = [False]
 
-    heads_order = [quad_member[1], quad_member[2], quad_member[0], member]
-
-    def attend(dy, then=None):
+    def attend(dy):
         tick_through(dy)
         if not quad_ready[0]:
             quad_ready[0] = True
             for i in range(3):
                 arrived(qall.at[quad_member[i]], q_r.at[i])
 
-        def masks():
+        @pl.when(y >= dy)
+        def _():
             key_pos = ((y - dy) * 4 + col_i // PIECE) * TOK + member * PIECE + col_i % PIECE
             keep = (key_pos <= first + row_i) & (prompt(key_pos) == pid_row)
-            bias[...] = jnp.where(keep, 0.0, MASKED)
-
-        def one(hh):
+            bias = jnp.where(keep, 0.0, MASKED)
             keys = kv[dy, 0].reshape(TOK, HD)
-            s = dot(keys, qall[hh], NT) + bias[...]
-            old = stat[hh, 0:1]
-            new = jnp.maximum(old, jnp.max(s, axis=0, keepdims=True))
-            scale = jnp.exp(old - new)
-            p = jnp.exp(s - new)
-            stat[hh, 0:1] = new
-            stat[hh, 1:2] = stat[hh, 1:2] * scale + jnp.sum(p, axis=0, keepdims=True)
             vals_t = kv[dy, 1].reshape(TOK, HD).T
-            acc[hh] = acc[hh] * scale + dot(vals_t, p.astype(BF16))
-
-        pl.when(y >= dy)(masks)
-        for n, hh in enumerate(heads_order):
-            pl.when(y >= dy)(functools.partial(one, hh))
-            if then is not None:
-                then(n)
-            else:
-                tick()
-
+            for hh in range(4):
+                s = dot(keys, qall[hh], NT) + bias
+                top = jnp.max(s, axis=0, keepdims=True)
+                if dy == 0:
+                    new = jnp.maximum(top, START_MAX)
+                    p = jnp.exp(s - new)
+                    stat[hh, 1:2] = jnp.sum(p, axis=0, keepdims=True)
+                    acc[hh] = dot(vals_t, p.astype(BF16))
+                else:
+                    old = stat[hh, 0:1]
+                    new = jnp.maximum(old, top)
+                    scale = jnp.exp(old - new)
+                    p = jnp.exp(s - new)
+                    stat[hh, 1:2] = stat[hh, 1:2] * scale + jnp.sum(p, axis=0, keepdims=True)
+                    acc[hh] = acc[hh] * scale + dot(vals_t, p.astype(BF16))
+                stat[hh, 0:1] = new
+
+    tick()
+    fold(0, z % 2 == 0)
+    z_exchange(1).start()
     attend(0)
-    chain_wait(0, 1)
-    chain_wait(1, 2)
-    for h in range(2):
-        pack(1, h, *compose(unpack(crecv[0, h]), unpack(crecv[1, h])))
-    chain_start(1, 2, 2)
+    tick(3)
+    fold(1, z < 2)
+    hop_start(0)
+    tick(2)
     attend(1)
-    chain_wait(2, 2)
-    for h in range(2):
-        pack(2, h, *compose(unpack(csend[1, h]), unpack(crecv[2, h])))
-    chain_start(2, 3, 4)
+    hop_wait(0)
+    hop_start(1)
+    tick(2)
     attend(2)
-    chain_wait(3, 4)
-    for h in range(2):
-        pack(3, h, *compose(unpack(csend[2, h]), unpack(crecv[3, h])))
-    chain_start(3, 4, 8)
+    hop_wait(1)
+    hop_start(2)
+    tick(4)
+    hop_wait(2)
+    hop_start(3)
     attend(3)
+    hop_wait(3)
+    share_start()
+    attend(4)
+
+    def partial(i):
+        return accs.at[i], accr.at[i], a_s.at[i], a_r.at[i], (xn_grp if i == 2 else sib_grp), ctx
+
+    def partial_stats(i):
+        return stats.at[i], statr.at[i], t_s.at[i], t_r.at[i], (xn_grp if i == 2 else sib_grp), ctx
+
+    for i, m in ((1, quad_member[2]), (0, quad_member[0])):
+        accs[i] = acc[m].astype(BF16)
+        stats[i] = stat[m]
+        copy(*partial_stats(i)).start()
+        copy(*partial(i)).start()
 
     def project(p, heads, w_ref):
         for b in range(8):
@@ -425,28 +493,46 @@
             i = p * 8 + b
             copy(pbuf.at[p, 1 - c, b], r1.at[p, b], s1_s.at[i], s1_r.at[i], sib_grp, ctx).start()
 
-    def pair_sum(p, b):
-        arrived(r1.at[p, b], s1_r.at[p * 8 + b])
-        return pbuf[p, c, b].astype(F32) + r1[p, b].astype(F32)
-
-    def across_x(p):
-        for d in (2, 1, 3):
-            xd = (x + d) % 4
+    half = [pl.ds(0, TOK // 2), pl.ds(TOK // 2, TOK // 2)]
+    step1_grp, step2_grp = [xn_grp, xm_grp], [xm_grp, xn_grp]
+    step1_x, step2_x = [xn, xm], [xm, xn]
+
+    def pair_half(p, b, a):
+        return pbuf[p, c, b, half[a]].astype(F32) + r1[p, b, half[a]].astype(F32)
+
+    def copy_x1(p, a):
+        i = p * 2 + a
+        return copy(s2.at[p, a], r2.at[p, a], s2_s.at[i], s2_r.at[i], step1_grp[a], ctx)
+
+    def copy_x2(p, a):
+        i = 4 + p * 2 + a
+        return copy(s4.at[p, a], r4.at[p, a], s2_s.at[i], s2_r.at[i], step2_grp[a], ctx)
+
+    def across_x1(p):
+        for b in range(8):
+            arrived(r1.at[p, b], s1_r.at[p * 8 + b])
+        for a in range(2):
             for e in range(2):
-                s2[p, d - 1, e] = pair_sum(p, xd * 2 + e).astype(BF16)
-            i = p * 3 + d - 1
-            copy(s2.at[p, d - 1], r2.at[p, d - 1], s2_s.at[i], s2_r.at[i], x_grp[d - 1], ctx).start()
+                s2[p, a, 0, e] = pair_half(p, step1_x[a] * 2 + e, a).astype(BF16)
+                s2[p, a, 1, e] = pair_half(p, xo * 2 + e, a).astype(BF16)
+            copy_x1(p, a).start()
+
+    def across_x2(p):
+        for a in range(2):
+            arrived(r2.at[p, a], s2_r.at[p * 2 + a])
+            for e in range(2):
+                s4[p, a, e] = (pair_half(p, step2_x[a] * 2 + e, a) + r2[p, a, 1, e].astype(F32)).astype(BF16)
+            copy_x2(p, a).start()
 
     def across_z(p):
-        far = pair_sum(p, x * 2 + 1 - zh)
-        near = pair_sum(p, x * 2 + zh)
-        for d in (1, 3, 2):
-            arrived(r2.at[p, d - 1], s2_r.at[p * 3 + d - 1])
-            far += r2[p, d - 1, 1 - zh].astype(F32)
-            near += r2[p, d - 1, zh].astype(F32)
-        s3[p] = far.astype(BF16)
+        near = []
+        for a in range(2):
+            arrived(r4.at[p, a], s2_r.at[4 + p * 2 + a])
+            far = pair_half(p, x * 2 + 1 - zh, a) + r2[p, a, 0, 1 - zh].astype(F32) + r4[p, a, 1 - zh].astype(F32)
+            s3[p, half[a]] = far.astype(BF16)
+            near.append(pair_half(p, x * 2 + zh, a) + r2[p, a, 0, zh].astype(F32) + r4[p, a, zh].astype(F32))
         copy(s3.at[p], r3.at[p], s3_s.at[p], s3_r.at[p], z_grp, ctx).start()
-        return near
+        return jnp.concatenate(near, axis=0)
 
     def finish(p, near, o_ref):
         arrived(r3.at[p], s3_r.at[p])
@@ -454,49 +540,55 @@
 
     for load in (loads[9], loads[11]):
         load.wait()
-    chain_wait(4, 8)
+    share_wait()
     heads = []
     for h in range(2):
-        state = apply_map(unpack(csend[3, h]), crecv[4, h, DHD : 2 * DHD])
-        core = dot3(split(eff[h, :, :DHD]), split(state)) + eff[h, :, DHD:]
+        e_hi, e_lo = split(eff[h, :, :DHD])
+        core = dot(e_hi, state[h], NT) + dot(e_lo, state[h], NT) + eff[h, :, DHD:]
         squares = jnp.mean(core * core, axis=1, keepdims=True)
         gate = dgate_ref[:, h * DHD : (h + 1) * DHD].astype(F32)
         normed = core * lax.rsqrt(squares + EPS) * gain_ref[...]
         heads.append((normed * gate * jax.nn.sigmoid(gate)).astype(BF16))
     project(1, jnp.concatenate(heads, axis=1), wd_ref)
-    tick(4)
-
-    def send_partial(n):
-        if n == 3:
-            return
-        i = (1, 2, 0)[n]
-        accs[i] = acc[quad_member[i]].astype(BF16)
-        stats[i] = stat[quad_member[i]]
-        copy(stats.at[i], statr.at[i], t_s.at[i], t_r.at[i], quad_grp[i], ctx).start()
-        copy(accs.at[i], accr.at[i], a_s.at[i], a_r.at[i], quad_grp[i], ctx).start()
-
-    attend(4, send_partial)
-    across_x(1)
+    def joined(accs_, stats_):
+        top = stats_[0][0:1]
+        for st in stats_[1:]:
+            top = jnp.maximum(top, st[0:1])
+        mixed, total = 0.0, 0.0
+        for ac, st in zip(accs_, stats_):
+            scale = jnp.exp(st[0:1] - top)
+            mixed += ac.astype(F32) * scale
+            total += st[1:2] * scale
+        return mixed, top, total
+
+    for i in (1, 0):
+        arrived(statr.at[i], t_r.at[i])
+        arrived(accr.at[i], a_r.at[i])
+    for i, m in ((2, quad_member[1]), (3, member)):
+        mixed, top, total = joined([acc[m], accr[3 - i]], [stat[m], statr[3 - i]])
+        if i == 2:
+            accs[i] = mixed.astype(BF16)
+            stats[i, 0:1] = top
+            stats[i, 1:2] = total
+            copy(*partial_stats(i)).start()
+            copy(*partial(i)).start()
+        else:
+            acc[m] = mixed
+            stat[m, 0:1] = top
+            stat[m, 1:2] = total
+    across_x1(1)
     for load in (loads[10], loads[12]):
         load.wait()
-    for i in range(3):
-        arrived(statr.at[i], t_r.at[i])
-    top = stat[member, 0:1]
-    for i in range(3):
-        top = jnp.maximum(top, statr[i, 0:1])
-    scale = jnp.exp(stat[member, 0:1] - top)
-    total = stat[member, 1:2] * scale
-    mixed = acc[member] * scale
-    for i in (0, 1, 2):
-        arrived(accr.at[i], a_r.at[i])
-        scale = jnp.exp(statr[i, 0:1] - top)
-        total += statr[i, 1:2] * scale
-        mixed += accr[i].astype(F32) * scale
+    arrived(statr.at[2], t_r.at[2])
+    arrived(accr.at[2], a_r.at[2])
+    mixed, _, total = joined([acc[member], accr[2]], [stat[member], statr[2]])
     core_out = (mixed / total).T
     attn_heads = (core_out * jax.nn.sigmoid(agate_ref[...].astype(F32))).astype(BF16)
     project(0, attn_heads, wa_ref)
+    across_x2(1)
+    across_x1(0)
     near_d = across_z(1)
-    across_x(0)
+    across_x2(0)
     finish(1, near_d, od_ref)
     near_a = across_z(0)
     finish(0, near_a, oa_ref)
@@ -504,8 +596,8 @@
     for i in range(3):
         copy(kv.at[0, :, z], kv.at[0, :, z], z_s.at[i], kv_r.at[z], grp, row_ctx[i]).wait_send()
         copy(qall.at[member], qall.at[member], q_s.at[i], q_r.at[i], quad_grp[i], ctx).wait_send()
-        copy(stats.at[i], statr.at[i], t_s.at[i], t_r.at[i], quad_grp[i], ctx).wait_send()
-        copy(accs.at[i], accr.at[i], a_s.at[i], a_r.at[i], quad_grp[i], ctx).wait_send()
+        copy(*partial_stats(i)).wait_send()
+        copy(*partial(i)).wait_send()
     for dy in range(4):
 
         @pl.when((y >= dy) & (y < 7))
@@ -513,19 +605,23 @@
             for zs in range(4):
                 forward(dy, zs).wait_send()
 
-    for step, slot, distance in ((0, 0, 1), (0, 1, 2), (1, 2, 2), (2, 3, 4), (3, 4, 8)):
-
-        @pl.when(ctx + distance < 32)
-        def _():
-            chain_send(step, slot, distance).wait_send()
+    for step in range(2):
+        z_exchange(step).wait_send()
+    for d in range(3):
+        share(d).wait_send()
+
+    @pl.when(y < 7)
+    def _():
+        for k in range(4):
+            row_hop(k).wait_send()
 
     for p in range(2):
         for b in range(8):
             i = p * 8 + b
             copy(pbuf.at[p, 1 - c, b], r1.at[p, b], s1_s.at[i], s1_r.at[i], sib_grp, ctx).wait_send()
-        for d in range(3):
-            i = p * 3 + d
-            copy(s2.at[p, d], r2.at[p, d], s2_s.at[i], s2_r.at[i], x_grp[d], ctx).wait_send()
+        for a in range(2):
+            copy_x1(p, a).wait_send()
+            copy_x2(p, a).wait_send()
         copy(s3.at[p], r3.at[p], s3_s.at[p], s3_r.at[p], z_grp, ctx).wait_send()
 
 
@@ -568,21 +664,25 @@
             pltpu.VMEM((256, 2048), BF16),
             pltpu.VMEM((4, TOK, HD), BF16),
             pltpu.VMEM((5, 2, 4, PIECE, HD), BF16),
-            pltpu.VMEM((TOK, TOK), F32),
             pltpu.VMEM((4, HD, TOK), F32),
             pltpu.VMEM((4, 8, TOK), F32),
             pltpu.VMEM((3, HD, TOK), BF16),
             pltpu.VMEM((3, HD, TOK), BF16),
             pltpu.VMEM((3, 8, TOK), F32),
             pltpu.VMEM((3, 8, TOK), F32),
-            pltpu.VMEM((2, MSG, DHD), F32),
-            pltpu.VMEM((4, 2, MSG, DHD), BF16),
-            pltpu.VMEM((5, 2, MSG, DHD), BF16),
+            pltpu.VMEM((3, 2, MSG, DHD), BF16),
+            pltpu.VMEM((2, 2, MSG, DHD), BF16),
+            pltpu.VMEM((4, 2, QUARTER, DHD), BF16),
+            pltpu.VMEM((4, 2, QUARTER, DHD), BF16),
+            pltpu.VMEM((2, DHD, DHD), BF16),
+            pltpu.VMEM((2, DHD, DHD), BF16),
             pltpu.VMEM((2, TOK, 2 * DHD), F32),
             pltpu.VMEM((2, 2, 8, TOK, DHD), BF16),
             pltpu.VMEM((2, 8, TOK, DHD), BF16),
-            pltpu.VMEM((2, 3, 2, TOK, DHD), BF16),
-            pltpu.VMEM((2, 3, 2, TOK, DHD), BF16),
+            pltpu.VMEM((2, 2, 2, 2, TOK // 2, DHD), BF16),
+            pltpu.VMEM((2, 2, 2, 2, TOK // 2, DHD), BF16),
+            pltpu.VMEM((2, 2, 2, TOK // 2, DHD), BF16),
+            pltpu.VMEM((2, 2, 2, TOK // 2, DHD), BF16),
             pltpu.VMEM((2, TOK, DHD), BF16),
             pltpu.VMEM((2, TOK, DHD), BF16),
             dma(13),
@@ -591,16 +691,20 @@
             dma(3),
             dma(16),
             dma(20),
-            dma(5),
-            dma(5),
+            dma(2),
+            dma(2),
+            dma(4),
+            dma(4),
+            dma(3),
+            dma(3),
             dma(3),
             dma(3),
             dma(3),
             dma(3),
             dma(16),
             dma(16),
-            dma(6),
-            dma(6),
+            dma(8),
+            dma(8),
             dma(2),
             dma(2),
         ],

time: 83.6 us -> 77.8 us (0.931)
  the two profiles are of different devices: /device:TPU:104 before, /device:TPU:56 now
where the time goes in v3:
time: 77.8 us; the launch traced here: 77.6 us
  Pallas kernels  74.8 us (96%)
  local copies, waits for them, and re-layouts  2.14 us (3%)
    pallas_call x1, Pallas kernels, local(): pl.pallas_call(kernel, out_shape=(out, out), in_specs=[pl.BlockSpec(memor...  74.8 us
    unnamed x4, local copies, waits for them, and re-layouts  2.14 us

profile of v3, /device:TPU:56, one launch (start us, length us, event | category | flops | bytes accessed | tf_op | source)
XLA Modules:
  0.0 77.6 jit_solution(8985911234999064133)
XLA Ops:
  0.6 74.8 %shard_map.149 = (bf16[256,128]{1,0:T(8,128)(2,1)}, bf16[256,128]{1,0:T(8,128)(2,1)}) custom-call(s32[4]{0:T(128)} %lengths_ref.1, bf16[256,256]{1,0:T(8,128)(2,1)} %q_hbm.1, bf16[256,512]{1,0:T(8,128)(2,1)} %k_hbm.1, bf16[256,512]{1,0:T(8,128)(2,1)} %v_hbm.1, bf16[256,256]{1,0:T(8,128)(2,1)} %agate_hbm.1, bf16[256,128]{1,0:T(8,128)(2,1)} %dq_hbm.1, ...), custom_call_target="tpu_custom_call" | custom-call | flops 4000000000 | bytes 6000000 | tf_op jit(solution)/shard_map/pallas_call | solution.py:648
  75.5 0.0 copy-start
  75.5 1.5 %copy.18 = bf16[256,128]{1,0:T(8,128)(2,1)} copy(bf16[256,128]{1,0:T(8,128)(2,1)} %get-tuple-element.4) | data formatting | bytes 131072
  77.0 0.0 copy-done
  77.0 0.6 copy.19
Async XLA Ops:
  75.5 1.5 %copy-start = (bf16[256,128]{1,0:T(8,128)(2,1)S(1)}, bf16[256,128]{1,0:T(8,128)(2,1)}, u32[]{:S(2)}) copy-start(bf16[256,128]{1,0:T(8,128)(2,1)} %get-tuple-element.5) | copy-start | bytes 196612

commit v4 on v3

--- a/solution.py
+++ b/solution.py
@@ -209,14 +209,14 @@
     for i in (1, 2, 0):
         copy(qall.at[member], qall.at[member], q_s.at[i], q_r.at[i], quad_grp[i], ctx).start()
 
-    ticks = [(1, 0), (0, 1), (0, 2), (0, 3)] + [(dy, i) for dy in range(1, 5) for i in range(4)][1:]
+    ticks = [(0, 1), (1, 0), (0, 2), (0, 3)] + [(dy, i) for dy in range(1, 5) for i in range(4)][1:]
 
     def tick(count=1):
         for _ in range(count):
             if not ticks:
                 return
             dy, i = ticks.pop(0)
-            zs = (z + i) % 4
+            zs = (z + 4 - i) % 4
 
             @pl.when(y >= dy)
             def _():
@@ -294,7 +294,7 @@
             parts = [split(t) for t in inverses]
             inner = [dot3(split(jnp.where(cross, low, 0.0)), t) for low, t in zip(lows, parts)]
             inverses = [t - dot3(tp, split(m)) for t, tp, m in zip(inverses, parts, inner)]
-            if size == 128:
+            if size >= 64:
                 tick()
         size *= 2
 
@@ -462,15 +462,16 @@
     hop_wait(0)
     hop_start(1)
     tick(2)
-    attend(2)
     hop_wait(1)
     hop_start(2)
-    tick(4)
+    tick(2)
+    attend(2)
     hop_wait(2)
     hop_start(3)
-    attend(3)
+    tick(2)
     hop_wait(3)
     share_start()
+    attend(3)
     attend(4)
 
     def partial(i):
@@ -549,7 +550,6 @@
         gate = dgate_ref[:, h * DHD : (h + 1) * DHD].astype(F32)
         normed = core * lax.rsqrt(squares + EPS) * gain_ref[...]
         heads.append((normed * gate * jax.nn.sigmoid(gate)).astype(BF16))
-    project(1, jnp.concatenate(heads, axis=1), wd_ref)
     def joined(accs_, stats_):
         top = stats_[0][0:1]
         for st in stats_[1:]:
@@ -576,6 +576,7 @@
             acc[m] = mixed
             stat[m, 0:1] = top
             stat[m, 1:2] = total
+    project(1, jnp.concatenate(heads, axis=1), wd_ref)
     across_x1(1)
     for load in (loads[10], loads[12]):
         load.wait()

time: 77.8 us -> 75.5 us (0.970)
  Pallas kernels: 74.8 us -> 72.6 us
    pallas_call x1, Pallas kernels: 74.8 us -> 72.6 us  [local(): pl.pallas_call(kernel, out_shape=(out, out), in_specs=[pl.BlockSpec(memor...]
where the time goes in v4:
time: 75.5 us; the launch traced here: 75.4 us
  Pallas kernels  72.6 us (96%)
  local copies, waits for them, and re-layouts  2.14 us (3%)
    pallas_call x1, Pallas kernels, local(): pl.pallas_call(kernel, out_shape=(out, out), in_specs=[pl.BlockSpec(memor...  72.6 us
    unnamed x4, local copies, waits for them, and re-layouts  2.14 us

profile of v4, /device:TPU:56, one launch (start us, length us, event | category | flops | bytes accessed | tf_op | source)
XLA Modules:
  0.0 75.4 jit_solution(2299148460023533536)
XLA Ops:
  0.6 72.6 %shard_map.149 = (bf16[256,128]{1,0:T(8,128)(2,1)}, bf16[256,128]{1,0:T(8,128)(2,1)}) custom-call(s32[4]{0:T(128)} %lengths_ref.1, bf16[256,256]{1,0:T(8,128)(2,1)} %q_hbm.1, bf16[256,512]{1,0:T(8,128)(2,1)} %k_hbm.1, bf16[256,512]{1,0:T(8,128)(2,1)} %v_hbm.1, bf16[256,256]{1,0:T(8,128)(2,1)} %agate_hbm.1, bf16[256,128]{1,0:T(8,128)(2,1)} %dq_hbm.1, ...), custom_call_target="tpu_custom_call" | custom-call | flops 4000000000 | bytes 6000000 | tf_op jit(solution)/shard_map/pallas_call | solution.py:649
  73.2 0.0 copy-start
  73.2 1.5 %copy.18 = bf16[256,128]{1,0:T(8,128)(2,1)} copy(bf16[256,128]{1,0:T(8,128)(2,1)} %get-tuple-element.4) | data formatting | bytes 131072
  74.7 0.0 copy-done
  74.7 0.6 copy.19
Async XLA Ops:
  73.2 1.5 %copy-start = (bf16[256,128]{1,0:T(8,128)(2,1)S(1)}, bf16[256,128]{1,0:T(8,128)(2,1)}, u32[]{:S(2)}) copy-start(bf16[256,128]{1,0:T(8,128)(2,1)} %get-tuple-element.5) | copy-start | bytes 196612

commit v5 on v4

--- a/solution.py
+++ b/solution.py
@@ -290,6 +290,15 @@
         cross = (ii // (2 * size) == jj // (2 * size)) & (ii // size != jj // size)
         if size == 1:
             inverses = [eye - jnp.where(cross, low, 0.0) for low in lows]
+        elif size == TOK // 2:
+            joined_up = []
+            for low, t in zip(lows, inverses):
+                above, below = t[:size, :size], t[size:, size:]
+                inner = dot3(split(low[size:, :size]), split(above))
+                corner = -dot3(split(below), split(inner))
+                joined_up.append(jnp.concatenate([t[:size], jnp.concatenate([corner, below], axis=1)], axis=0))
+            inverses = joined_up
+            tick()
         else:
             parts = [split(t) for t in inverses]
             inner = [dot3(split(jnp.where(cross, low, 0.0)), t) for low, t in zip(lows, parts)]

time: 75.5 us -> 75.4 us (level)
  no operation moved by 1% of the time
where the time goes in v5:
time: 75.4 us; the launch traced here: 75.2 us
  Pallas kernels  72.4 us (96%)
  local copies, waits for them, and re-layouts  2.14 us (3%)
    pallas_call x1, Pallas kernels, local(): pl.pallas_call(kernel, out_shape=(out, out), in_specs=[pl.BlockSpec(memor...  72.4 us
    unnamed x4, local copies, waits for them, and re-layouts  2.14 us

profile of v5, /device:TPU:56, one launch (start us, length us, event | category | flops | bytes accessed | tf_op | source)
XLA Modules:
  0.0 75.2 jit_solution(11086553839013858101)
XLA Ops:
  0.6 72.4 %shard_map.149 = (bf16[256,128]{1,0:T(8,128)(2,1)}, bf16[256,128]{1,0:T(8,128)(2,1)}) custom-call(s32[4]{0:T(128)} %lengths_ref.1, bf16[256,256]{1,0:T(8,128)(2,1)} %q_hbm.1, bf16[256,512]{1,0:T(8,128)(2,1)} %k_hbm.1, bf16[256,512]{1,0:T(8,128)(2,1)} %v_hbm.1, bf16[256,256]{1,0:T(8,128)(2,1)} %agate_hbm.1, bf16[256,128]{1,0:T(8,128)(2,1)} %dq_hbm.1, ...), custom_call_target="tpu_custom_call" | custom-call | flops 4000000000 | bytes 6000000 | tf_op jit(solution)/shard_map/pallas_call | solution.py:658
  73.1 0.0 copy-start
  73.1 1.5 %copy.18 = bf16[256,128]{1,0:T(8,128)(2,1)} copy(bf16[256,128]{1,0:T(8,128)(2,1)} %get-tuple-element.4) | data formatting | bytes 131072
  74.6 0.0 copy-done
  74.6 0.6 copy.19
Async XLA Ops:
  73.1 1.5 %copy-start = (bf16[256,128]{1,0:T(8,128)(2,1)S(1)}, bf16[256,128]{1,0:T(8,128)(2,1)}, u32[]{:S(2)}) copy-start(bf16[256,128]{1,0:T(8,128)(2,1)} %get-tuple-element.5) | copy-start | bytes 196612
